TPU v7x, 32 devices: a whole 2x2x4 slice. The times are simulated.
32 devices in a mesh: ctx: 8 (over z, x), head: 4 (over y, core).
Axes of the slice: x: 2, y: 2, z: 4, core: 2. Of those that a mesh axis runs over, the one named last changes fastest.
Arguments:
- query_in: bfloat16 [4096, 2048], P('ctx', 'head'), may hold values from -6 to 6
- key_in: bfloat16 [4096, 2048], P('ctx', 'head'), may hold values from -6 to 6
- value_in: bfloat16 [4096, 4096], P('ctx', 'head'), may hold values from -6 to 6
- query_taps: float32 [4, 2048], P(None, 'head'), may hold values from -3 to 3
- key_taps: float32 [4, 2048], P(None, 'head'), may hold values from -3 to 3
- value_taps: float32 [4, 4096], P(None, 'head'), may hold values from -3 to 3
- log_decay: float32 [32, 4096], P('head', 'ctx'), may hold values from -2 to 0
- beta_logit: float32 [32, 4096], P('head', 'ctx'), may hold values from -9 to 2
- gate_in: bfloat16 [4096, 4096], P('ctx', 'head'), may hold values from -6 to 6
- norm_gain: float32 [128], replicated, may hold values from 0.1 to 1.9
Outputs:
- core_out: bfloat16 [4096, 4096], P(('ctx', 'head'))
All inputs are finite; a program needn't handle non-finite values.
Results may differ from a plain program's by a relative error of at most 0.005.
Values may be sent and summed in bfloat16 or wider, within the bound.
A program may use at most 64 MiB of HBM per device.

v0:
```python
import jax
import jax.numpy as jnp
from jax import lax
from jax.sharding import PartitionSpec as P

GROUP = 64


highest = lax.Precision.HIGHEST
norm_eps = 1e-06


def shifted(value, axis, steps):
    count = lax.axis_size(axis)
    first, last = (max(0, -steps), min(count, count - steps))
    return lax.ppermute(value, axis, [(source, source + steps) for source in range(first, last)])


def causal_conv(joined, taps, length):
    summed = jnp.zeros((length, joined.shape[1]), jnp.float32)
    for offset in range(taps.shape[0]):
        summed = summed + taps[offset] * joined[offset : offset + length].astype(jnp.float32)
    return jax.nn.silu(summed)


def unit_rows(matrix):
    return matrix * lax.rsqrt(jnp.sum(matrix * matrix, axis=-1, keepdims=True) + norm_eps)


def group_terms(query, keys, values, beta, logdecay):
    length = logdecay.shape[-1]
    cumul = jnp.cumsum(logdecay, axis=-1)
    row_ids = lax.broadcasted_iota(jnp.int32, (length, length), 0)
    col_ids = lax.broadcasted_iota(jnp.int32, (length, length), 1)
    inside = col_ids <= row_ids
    differ = cumul[..., :, None] - cumul[..., None, :]
    decay_mask = jnp.where(inside, jnp.exp(jnp.where(inside, differ, 0.0)), 0.0)
    keygram = jnp.einsum("...ik,...jk->...ij", keys, keys, precision=highest)
    strict = jnp.where(col_ids < row_ids, beta[..., :, None] * keygram * decay_mask, 0.0)
    identity_mats = jnp.broadcast_to(jnp.eye(length, dtype=jnp.float32), strict.shape)
    inverse = lax.linalg.triangular_solve(
        identity_mats + strict, identity_mats, left_side=True, lower=True, unit_diagonal=True
    )
    upd_values = jnp.einsum(
        "...ij,...jd->...id", inverse, beta[..., None] * values, precision=highest
    )
    upd_keys = jnp.einsum(
        "...ij,...jd->...id", inverse, (beta * jnp.exp(cumul))[..., None] * keys, precision=highest
    )
    scores = jnp.einsum("...ik,...jk->...ij", query, keys, precision=highest) * decay_mask
    last_log = cumul[..., -1:]
    query_decay = query * jnp.exp(cumul)[..., None]
    key_decay = keys * jnp.exp(last_log - cumul)[..., None]
    return (upd_values, upd_keys, scores, query_decay, key_decay, last_log[..., 0])


def group_step(state, terms):
    upd_values, upd_keys, scores, query_decay, key_decay, last_log = terms
    new_values = upd_values - jnp.einsum("...ik,...kd->...id", upd_keys, state, precision=highest)
    output = jnp.einsum("...ik,...kd->...id", query_decay, state, precision=highest)
    output = output + jnp.einsum("...ij,...jd->...id", scores, new_values, precision=highest)
    state = jnp.exp(last_log)[..., None, None] * state + jnp.einsum(
        "...ik,...id->...kd", key_decay, new_values, precision=highest
    )
    return (state, output)


def matmul_pair(left_mats, right_mats):
    return jnp.einsum("...ij,...jk->...ik", left_mats, right_mats, precision=highest)


def body(
    query_in,
    key_in,
    value_in,
    query_taps,
    key_taps,
    value_taps,
    log_decay,
    beta_logit,
    gate_in,
    norm_gain,
):
    head_size = norm_gain.shape[0]
    length = query_in.shape[0]
    value_heads = log_decay.shape[0]
    key_heads = query_in.shape[1] // head_size
    share_ratio = value_heads // key_heads
    rim_width = query_taps.shape[0] - 1
    groups_dev = length // GROUP
    tail_rows = shifted(
        (
            query_in[length - rim_width :],
            key_in[length - rim_width :],
            value_in[length - rim_width :],
        ),
        "ctx",
        1,
    )
    query_conv = causal_conv(jnp.concatenate([tail_rows[0], query_in], axis=0), query_taps, length)
    key_conv = causal_conv(jnp.concatenate([tail_rows[1], key_in], axis=0), key_taps, length)
    value_conv = causal_conv(jnp.concatenate([tail_rows[2], value_in], axis=0), value_taps, length)
    queries = (
        unit_rows(query_conv.reshape(length, key_heads, head_size)) * head_size ** (-0.5)
    ).astype(jnp.bfloat16)
    keys = unit_rows(key_conv.reshape(length, key_heads, head_size)).astype(jnp.bfloat16)
    values = value_conv.reshape(length, value_heads, head_size).astype(jnp.bfloat16)

    def blocked(array):
        return (
            array.astype(jnp.float32)
            .reshape(groups_dev, GROUP, array.shape[1], head_size)
            .transpose(0, 2, 1, 3)
        )

    def blocked_rates(array):
        return array.reshape(value_heads, groups_dev, GROUP).transpose(1, 0, 2)

    query_blocks = blocked(jnp.repeat(queries, share_ratio, axis=1))
    key_blocks = blocked(jnp.repeat(keys, share_ratio, axis=1))
    value_blocks = blocked(values)
    beta_blocks = blocked_rates(jax.nn.sigmoid(beta_logit))
    decay_blocks = blocked_rates(log_decay)
    terms = group_terms(query_blocks, key_blocks, value_blocks, beta_blocks, decay_blocks)
    upd_values, upd_keys, scores, query_decay, key_decay, last_log = terms
    identity_state = jnp.broadcast_to(
        jnp.eye(head_size, dtype=jnp.float32), (value_heads, head_size, head_size)
    )
    group_maps = jnp.exp(last_log)[..., None, None] * identity_state - jnp.einsum(
        "...ik,...ij->...kj", key_decay, upd_keys, precision=highest
    )
    query_effect = query_decay - matmul_pair(scores, upd_keys)

    def local_step(carry, packed):
        state, product = carry
        group, group_map = packed
        state, output = group_step(state, group)
        return ((state, matmul_pair(group_map, product)), output)

    zero_state = jnp.zeros((value_heads, head_size, head_size), jnp.float32)
    (local_state, shard_map_mat), local_out = lax.scan(
        local_step, (zero_state, identity_state), (terms, group_maps)
    )

    def chain_turn(turn, incoming_state):
        return shifted(matmul_pair(shard_map_mat, incoming_state) + local_state, "ctx", 1)

    incoming = lax.fori_loop(0, lax.axis_size("ctx") - 1, chain_turn, zero_state)

    def carried_step(state, packed):
        effect_group, group_map = packed
        return (matmul_pair(group_map, state), matmul_pair(effect_group, state))

    _, carried_out = lax.scan(carried_step, incoming, (query_effect, group_maps))
    output = (local_out + carried_out).transpose(0, 2, 1, 3).reshape(length, value_heads, head_size)
    gates = gate_in.reshape(length, value_heads, head_size).astype(jnp.float32)
    normed = (
        output
        * lax.rsqrt(jnp.mean(output * output, axis=-1, keepdims=True) + norm_eps)
        * norm_gain
        * jax.nn.silu(gates)
    )
    normed = normed.astype(jnp.bfloat16).reshape(length, value_heads * head_size)
    return lax.all_to_all(normed, "head", split_axis=0, concat_axis=1, tiled=True)


def solution(mesh):
    in_specs = (
        P("ctx", "head"),
        P("ctx", "head"),
        P("ctx", "head"),
        P(None, "head"),
        P(None, "head"),
        P(None, "head"),
        P("head", "ctx"),
        P("head", "ctx"),
        P("ctx", "head"),
        P(),
    )
    out_specs = P(("ctx", "head"), None)
    return jax.shard_map(body, mesh=mesh, in_specs=in_specs, out_specs=out_specs, check_vma=False)
```

profile of v0, /device:TPU:27, one launch (start us, length us, event | category | flops | bytes accessed | tf_op | source)
XLA Modules:
  0.0 604.9 jit_solution(17319840129878735896)
XLA Ops:
  6.9 1.8 reduce_window_sum.11
  12.5 2.7 divide_multiply_fusion.1
  18.1 2.7 add_bitcast_fusion.1
  20.9 315.2 %custom-call.3 = f32[8,8,1,64,64]{3,4,2,1,0:T(8,128)S(1)} custom-call(f32[8,8,1,64,64]{4,3,2,1,0:T(8,128)} %add_bitcast_fusion.1), custom_call_target="InvertDiagBlocksLowerTriangular" | custom-call | tf_op jit(solution)/shard_map/triangular_solve | solution.py:41
  336.1 4.8 fusion.43
  346.9 2.3 fusion.45
  349.3 4.0 convolution_subtract_fusion.1
  353.2 8.8 %multiply_subtract_fusion = f32[8,8,128,128]{3,2,1,0:T(8,128)} fusion(f32[8,8,64,128]{3,2,1,0:T(8,128)S(1)} %fusion.45, f32[128,128]{1,0:T(8,128)S(1)} %fusion.62, f32[8,8]{1,0:T(8,128)S(1)} %exp.60, f32[8,8,64,128]{3,2,0,1:T(8,128)S(1)} %get-tuple-element.230), kind=kOutput, calls=%fused_computation.43 | convolution fusion | flops 807403520 | bytes 8454400 | tf_op jit(solution)/shard_map/...ik,...ij->...kj/dot_general | solution.py:129
  362.0 1.7 convert_multiply_fusion.3
  363.7 1.6 copy.63
  365.3 1.6 convert_bitcast_fusion
  367.4 3.7 fusion.42
  372.7 71.9 %while.39 = (s32[]{:T(128)}, f32[8,128,128]{2,1,0:T(8,128)S(1)}, f32[8,128,128]{2,1,0:T(8,128)S(1)}, f32[8,8,64,128]{3,2,1,0:T(8,128)}, f32[8,8]{1,0:T(8,128)S(1...) while((s32[]{:T(128)}, f32[8,128,128]{2,1,0:T(8,128)S(1)}, ...), condition=%wide.region_4.5_spmd.clone, body=%wide.region_3.4_spmd.clone.sunk | while | flops 554434560 | bytes 7604992 | solution.py:141
  375.8 2.1 convolution_add_fusion.6
  378.0 1.7 fusion.124
  379.7 2.1 fusion.126
  384.9 2.1 convolution_add_fusion.6
  387.0 1.7 fusion.124
  388.7 2.1 fusion.126
  393.8 2.1 convolution_add_fusion.6
  396.0 1.7 fusion.124
  397.7 2.1 fusion.126
  402.8 2.1 convolution_add_fusion.6
  405.0 1.7 fusion.124
  406.7 2.1 fusion.126
  411.8 2.1 convolution_add_fusion.6
  413.9 1.7 fusion.124
  415.7 2.1 fusion.126
  420.8 2.1 convolution_add_fusion.6
  422.9 1.7 fusion.124
  424.7 2.0 fusion.126
  429.8 2.1 convolution_add_fusion.6
  431.9 1.7 fusion.124
  433.6 2.0 fusion.126
  438.8 2.1 convolution_add_fusion.6
  440.9 1.7 fusion.124
  442.6 2.1 fusion.126
  444.7 94.4 %while.37 = (s32[]{:T(128)}, f32[8,128,128]{2,1,0:T(8,128)S(1)}, f32[8,128,128]{2,1,0:T(8,128)S(1)}, f32[8,128,128]{2,1,0:T(8,128)S(1)}, s32[]{:T(128)}) while((s32[]{:T(128)}, f32[8,128,128]{2,1,0:T(8,128)S(1)}, f32[8,128,128]{2,1,0:T(8,128)S(1)}, f32[8,128,128]{2,1,0:T(8,128)S(1)}, s32[]{:T(128)}) %tuple.69), condition=%wide.region_6.7_spmd, body=%wide.region_5.6_spmd.sunk | while | flops 201457664 | bytes 4194405 | solution.py:148
  446.7 15.3 %collective-permute-done = f32[8,128,128]{2,1,0:T(8,128)S(1)} collective-permute-done((f32[8,128,128]{2,1,0:T(8,128)S(1)}, f32[8,128,128]{2,1,0:T(8,128)S(1)}, u32[]{:S(2)}, u32[]{:S(2)}) %collective-permute-start) | collective-permute-done | bytes 524320 | tf_op jit(solution)/shard_map/while/body/eval_jaxpr/ppermute | solution.py:16
  463.9 13.0 %collective-permute-done = f32[8,128,128]{2,1,0:T(8,128)S(1)} collective-permute-done((f32[8,128,128]{2,1,0:T(8,128)S(1)}, f32[8,128,128]{2,1,0:T(8,128)S(1)}, u32[]{:S(2)}, u32[]{:S(2)}) %collective-permute-start) | collective-permute-done | bytes 524320 | tf_op jit(solution)/shard_map/while/body/eval_jaxpr/ppermute | solution.py:16
  478.9 12.1 %collective-permute-done = f32[8,128,128]{2,1,0:T(8,128)S(1)} collective-permute-done((f32[8,128,128]{2,1,0:T(8,128)S(1)}, f32[8,128,128]{2,1,0:T(8,128)S(1)}, u32[]{:S(2)}, u32[]{:S(2)}) %collective-permute-start) | collective-permute-done | bytes 524320 | tf_op jit(solution)/shard_map/while/body/eval_jaxpr/ppermute | solution.py:16
  493.0 11.2 %collective-permute-done = f32[8,128,128]{2,1,0:T(8,128)S(1)} collective-permute-done((f32[8,128,128]{2,1,0:T(8,128)S(1)}, f32[8,128,128]{2,1,0:T(8,128)S(1)}, u32[]{:S(2)}, u32[]{:S(2)}) %collective-permute-start) | collective-permute-done | bytes 524320 | tf_op jit(solution)/shard_map/while/body/eval_jaxpr/ppermute | solution.py:16
  506.2 10.3 %collective-permute-done = f32[8,128,128]{2,1,0:T(8,128)S(1)} collective-permute-done((f32[8,128,128]{2,1,0:T(8,128)S(1)}, f32[8,128,128]{2,1,0:T(8,128)S(1)}, u32[]{:S(2)}, u32[]{:S(2)}) %collective-permute-start) | collective-permute-done | bytes 524320 | tf_op jit(solution)/shard_map/while/body/eval_jaxpr/ppermute | solution.py:16
  518.4 9.2 %collective-permute-done = f32[8,128,128]{2,1,0:T(8,128)S(1)} collective-permute-done((f32[8,128,128]{2,1,0:T(8,128)S(1)}, f32[8,128,128]{2,1,0:T(8,128)S(1)}, u32[]{:S(2)}, u32[]{:S(2)}) %collective-permute-start) | collective-permute-done | bytes 524320 | tf_op jit(solution)/shard_map/while/body/eval_jaxpr/ppermute | solution.py:16
  529.6 9.5 %collective-permute-done = f32[8,128,128]{2,1,0:T(8,128)S(1)} collective-permute-done((f32[8,128,128]{2,1,0:T(8,128)S(1)}, f32[8,128,128]{2,1,0:T(8,128)S(1)}, u32[]{:S(2)}, u32[]{:S(2)}) %collective-permute-start) | collective-permute-done | bytes 524320 | tf_op jit(solution)/shard_map/while/body/eval_jaxpr/ppermute | solution.py:16
  540.8 32.7 %while.38 = (s32[]{:T(128)}, f32[8,128,128]{2,1,0:T(8,128)S(1)}, f32[8,8,64,128]{3,2,1,0:T(8,128)}, f32[8,8,128,128]{3,2,1,0:T(8,128)}, f32[8,8,64,128]{3,2,1,0:T(8,128)}, /*index=5*/s32[]{:T(128)}) while((s32[]{:T(128)}, f32[8,128,128]{2,1,0:T(8,128)S(1)}, f32[8,8,64,128]{3,2,1,0:T(8,128)}, f32[8,8,128,128]{3,2,1,0:T(8,128)}, ...), condition=%wide.region_8.9_spmd, body=%wide.region_7.8_spmd.sunk | while | flops 301989888 | bytes 3671121 | solution.py:154
  540.8 2.3 fusion.112
  543.1 1.7 fusion.111
  544.8 2.3 fusion.112
  547.1 1.7 fusion.111
  548.9 2.3 fusion.112
  551.2 1.7 fusion.111
  552.9 2.3 fusion.112
  555.2 1.7 fusion.111
  557.0 2.3 fusion.112
  559.3 1.7 fusion.111
  561.0 2.3 fusion.112
  563.3 1.7 fusion.111
  565.1 2.3 fusion.112
  567.4 1.7 fusion.111
  569.1 2.3 fusion.112
  571.5 1.7 fusion.111
  573.4 2.8 multiply_reduce_fusion
  580.1 23.7 %all_to_all.19 = bf16[4,128,1024]{2,1,0:T(8,128)(2,1)S(1)} all-to-all(bf16[4,128,1024]{2,1,0:T(8,128)(2,1)S(1)} %bitcast.158), channel_id=1, replica_groups=mesh['ctx'=8,'head'=4] {'head'}, dimensions={0} | all-to-all | bytes 2097152 | tf_op jit(solution)/shard_map/all_to_all | solution.py:164
  (125 shorter events, 66.9 us)
Async XLA Ops:
  0.0 12.3 %copy-start = (f32[128]{0:T(128)S(1)}, f32[128]{0:T(128)}, u32[]{:S(2)}) copy-start(f32[128]{0:T(128)} %param.25) | copy-start | bytes 1540
  0.7 11.8 %collective-permute-start.1 = (bf16[3,512]{1,0:T(4,128)(2,1)S(1)}, bf16[3,512]{1,0:T(4,128)(2,1)S(1)}, u32[]{:S(2)}, u32[]{:S(2)}) collective-permute-start(bf16[3,512]{1,0:T(4,128)(2,1)S(1)} %slice.81), channel_id=1, source_target_pairs={{0,4},{4,8},{8,12},{12,16},{16,20},{20,24},{24,28},{1,5},{5,9},{9,... | collective-permute-start | bytes 9224 | tf_op jit(solution)/shard_map/ppermute | solution.py:16
  2.7 362.6 %collective-permute-start.2 = (bf16[3,1024]{1,0:T(4,128)(2,1)S(1)}, bf16[3,1024]{1,0:T(4,128)(2,1)S(1)}, u32[]{:S(2)}, u32[]{:S(2)}) collective-permute-start(bf16[3,1024]{1,0:T(4,128)(2,1)S(1)} %slice.89), channel_id=1, source_target_pairs={{0,4},{4,8},{8,12},{12,16},{16,20},{20,24},{24,28},{1,5},{5,9},{9,... | collective-permute-start | bytes 18440 | tf_op jit(solution)/shard_map/ppermute | solution.py:16
  4.7 336.2 %collective-permute-start.3 = (bf16[3,512]{1,0:T(4,128)(2,1)S(1)}, bf16[3,512]{1,0:T(4,128)(2,1)S(1)}, u32[]{:S(2)}, u32[]{:S(2)}) collective-permute-start(bf16[3,512]{1,0:T(4,128)(2,1)S(1)} %slice.97), channel_id=1, source_target_pairs={{0,4},{4,8},{8,12},{12,16},{16,20},{20,24},{24,28},{1,5},{5,9},{9,... | collective-permute-start | bytes 9224 | tf_op jit(solution)/shard_map/ppermute | solution.py:16
  17.1 1.0 copy-start.3
  336.1 4.8 copy-start.7
  342.6 1.2 copy-start.4
  344.6 4.7 copy-start.2
  344.6 2.3 copy-start.1
  363.7 1.6 copy-start.5
  445.4 16.6 %collective-permute-start = (f32[8,128,128]{2,1,0:T(8,128)S(1)}, f32[8,128,128]{2,1,0:T(8,128)S(1)}, u32[]{:S(2)}, u32[]{:S(2)}) collective-permute-start(f32[8,128,128]{2,1,0:T(8,128)S(1)} %convolution_add_fusion.5), channel_id=1, source_target_pairs={{0,4},{4,8},{8,12},{12,16},{16,20},{20,24},{24,28},{1,5},{5,9},{9,... | collective-permute-start | bytes 1572872 | tf_op jit(solution)/shard_map/while/body/eval_jaxpr/ppermute | solution.py:16
  462.6 14.3 %collective-permute-start = (f32[8,128,128]{2,1,0:T(8,128)S(1)}, f32[8,128,128]{2,1,0:T(8,128)S(1)}, u32[]{:S(2)}, u32[]{:S(2)}) collective-permute-start(f32[8,128,128]{2,1,0:T(8,128)S(1)} %convolution_add_fusion.5), channel_id=1, source_target_pairs={{0,4},{4,8},{8,12},{12,16},{16,20},{20,24},{24,28},{1,5},{5,9},{9,... | collective-permute-start | bytes 1572872 | tf_op jit(solution)/shard_map/while/body/eval_jaxpr/ppermute | solution.py:16
  477.6 13.4 %collective-permute-start = (f32[8,128,128]{2,1,0:T(8,128)S(1)}, f32[8,128,128]{2,1,0:T(8,128)S(1)}, u32[]{:S(2)}, u32[]{:S(2)}) collective-permute-start(f32[8,128,128]{2,1,0:T(8,128)S(1)} %convolution_add_fusion.5), channel_id=1, source_target_pairs={{0,4},{4,8},{8,12},{12,16},{16,20},{20,24},{24,28},{1,5},{5,9},{9,... | collective-permute-start | bytes 1572872 | tf_op jit(solution)/shard_map/while/body/eval_jaxpr/ppermute | solution.py:16
  491.7 12.5 %collective-permute-start = (f32[8,128,128]{2,1,0:T(8,128)S(1)}, f32[8,128,128]{2,1,0:T(8,128)S(1)}, u32[]{:S(2)}, u32[]{:S(2)}) collective-permute-start(f32[8,128,128]{2,1,0:T(8,128)S(1)} %convolution_add_fusion.5), channel_id=1, source_target_pairs={{0,4},{4,8},{8,12},{12,16},{16,20},{20,24},{24,28},{1,5},{5,9},{9,... | collective-permute-start | bytes 1572872 | tf_op jit(solution)/shard_map/while/body/eval_jaxpr/ppermute | solution.py:16
  504.9 11.6 %collective-permute-start = (f32[8,128,128]{2,1,0:T(8,128)S(1)}, f32[8,128,128]{2,1,0:T(8,128)S(1)}, u32[]{:S(2)}, u32[]{:S(2)}) collective-permute-start(f32[8,128,128]{2,1,0:T(8,128)S(1)} %convolution_add_fusion.5), channel_id=1, source_target_pairs={{0,4},{4,8},{8,12},{12,16},{16,20},{20,24},{24,28},{1,5},{5,9},{9,... | collective-permute-start | bytes 1572872 | tf_op jit(solution)/shard_map/while/body/eval_jaxpr/ppermute | solution.py:16
  517.1 10.5 %collective-permute-start = (f32[8,128,128]{2,1,0:T(8,128)S(1)}, f32[8,128,128]{2,1,0:T(8,128)S(1)}, u32[]{:S(2)}, u32[]{:S(2)}) collective-permute-start(f32[8,128,128]{2,1,0:T(8,128)S(1)} %convolution_add_fusion.5), channel_id=1, source_target_pairs={{0,4},{4,8},{8,12},{12,16},{16,20},{20,24},{24,28},{1,5},{5,9},{9,... | collective-permute-start | bytes 1572872 | tf_op jit(solution)/shard_map/while/body/eval_jaxpr/ppermute | solution.py:16
  528.3 10.8 %collective-permute-start = (f32[8,128,128]{2,1,0:T(8,128)S(1)}, f32[8,128,128]{2,1,0:T(8,128)S(1)}, u32[]{:S(2)}, u32[]{:S(2)}) collective-permute-start(f32[8,128,128]{2,1,0:T(8,128)S(1)} %convolution_add_fusion.5), channel_id=1, source_target_pairs={{0,4},{4,8},{8,12},{12,16},{16,20},{20,24},{24,28},{1,5},{5,9},{9,... | collective-permute-start | bytes 1572872 | tf_op jit(solution)/shard_map/while/body/eval_jaxpr/ppermute | solution.py:16
  577.6 1.2 copy-start.6
where the time goes:
time: 612 us; the launch traced here: 605 us
  other arithmetic  333 us (54%)
  matrix products  135 us (22%)
  waiting for transfers between devices  80.6 us (13%)
  blocking collectives  23.7 us (4%)
  local copies, waits for them, and re-layouts  18.7 us (3%)
  starting transfers between devices  12.9 us (2%)
    another operation x3, other arithmetic, group_terms(): lax.linalg.triangular_solve(identity_mats + strict, identity_mats, left_s...  315 us
    ppermute x10, waiting for transfers between devices, shifted(): lax.ppermute(value, axis, [(source, source + steps) for source in range(f...  80.6 us
    dot_general x32, matrix products, matmul_pair(): jnp.einsum('...ij,...jk->...ik', left_mats, right_mats, precision=highest)  54.2 us
    all_to_all x1, blocking collectives, body(): lax.all_to_all(normed, 'head', split_axis=0, concat_axis=1, tiled=True)  23.7 us
    dot_general x8, matrix products, group_step(): jnp.einsum('...ij,...jd->...id', scores, new_values, precision=highest)  16.5 us
    dot_general x8, matrix products, group_step(): jnp.einsum('...ik,...id->...kd', key_decay, new_values, precision=highest)  16.4 us
    ppermute x10, starting transfers between devices, shifted(): lax.ppermute(value, axis, [(source, source + steps) for source in range(f...  12.9 us
    dot_general x8, matrix products, group_step(): jnp.einsum('...ik,...kd->...id', upd_keys, state, precision=highest)  12.3 us
  transfers between devices with their start and end apart: 10, of which 7 were waited for; matrix products, arithmetic and copies ran while one was open for 59% of the time, Pallas kernels for 0%

commit v1 on v0

v1 whole, which is shorter than its diff:
```python
import functools

import jax
import jax.numpy as jnp
from jax import lax
from jax.experimental import pallas as pl
from jax.experimental.pallas import tpu as pltpu
from jax.sharding import PartitionSpec as P

CHUNK = 128
PAD = 16
norm_eps = 1e-06
bf16 = jnp.bfloat16
f32 = jnp.float32
highest = lax.Precision.HIGHEST


def split(x):
    hi = x.astype(bf16)
    return hi, (x - hi.astype(f32)).astype(bf16)


def dot1(a, b):
    return jnp.dot(a, b, preferred_element_type=f32)


def dot3(a, b):
    (ah, al), (bh, bl) = a, b
    return dot1(jnp.concatenate([ah, al], axis=1), jnp.concatenate([bh, bh], axis=0)) + dot1(ah, bl)


def silu(x):
    return x / (1.0 + jnp.exp(-x))


def conv(buf, tail_ref, in_ref, taps_ref):
    length = in_ref.shape[0]
    count = taps_ref.shape[0]
    buf[0:PAD, :] = tail_ref[...].astype(f32)
    buf[PAD:, :] = in_ref[...].astype(f32)
    total = None
    for j in range(count):
        term = taps_ref[j : j + 1, :] * buf[pl.ds(PAD - count + 1 + j, length), :]
        total = term if total is None else total + term
    return silu(total)


def unit(x):
    return x * lax.rsqrt(jnp.sum(x * x, axis=-1, keepdims=True) + norm_eps)


def local_kernel(
    q_ref, k_ref, v_ref, qt_ref, kt_ref, vt_ref, qw_ref, kw_ref, vw_ref, ld_ref, bl_ref,
    out_ref, eff_ref, state_ref, prod_ref, qbuf, vbuf,
):
    length, dim = q_ref.shape
    ratio = v_ref.shape[1] // dim
    q_all = (unit(conv(qbuf, qt_ref, q_ref, qw_ref)) * dim ** (-0.5)).astype(bf16)
    k_all = unit(conv(qbuf, kt_ref, k_ref, kw_ref)).astype(bf16)
    v_all = conv(vbuf, vt_ref, v_ref, vw_ref).astype(bf16)

    size = CHUNK
    rows = lax.broadcasted_iota(jnp.int32, (size, size), 0)
    cols = lax.broadcasted_iota(jnp.int32, (size, size), 1)
    inside = cols <= rows
    strictly = cols < rows
    eye = jnp.where(cols == rows, 1.0, 0.0).astype(f32)
    upper = jnp.where(rows <= cols, 1.0, 0.0).astype(f32)
    masks = []
    width = 1
    while width < size:
        pick = (rows // (2 * width) == cols // (2 * width)) & (rows // width != cols // width)
        masks.append(jnp.where(pick & strictly, 1.0, 0.0).astype(bf16))
        width *= 2

    beta_all = 1.0 / (1.0 + jnp.exp(-bl_ref[0]))
    items = []
    for c in range(length // size):
        span = slice(c * size, (c + 1) * size)
        kc, qc = k_all[span], q_all[span]
        kf, qf = kc.astype(f32), qc.astype(f32)
        k_turn = kf.T
        nt = (((1,), (1,)), ((), ()))
        gram = lax.dot_general(kc, kc, nt, preferred_element_type=f32)
        qk = lax.dot_general(qc, kc, nt, preferred_element_type=f32)
        cum = lax.dot_general(
            ld_ref[0][:, span], upper, (((1,), (0,)), ((), ())),
            precision=highest, preferred_element_type=f32,
        )
        stacked = jnp.concatenate(
            [cum, beta_all[:, span], jnp.zeros((8 - 2 * ratio, size), f32)], axis=0
        )
        turned = stacked.T
        for h in range(ratio):
            cum_row = cum[h : h + 1]
            cum_col = turned[:, h : h + 1]
            beta_col = turned[:, ratio + h : ratio + h + 1]
            last = cum_row[:, size - 1 :]
            mask = jnp.where(inside, jnp.exp(jnp.where(inside, cum_col - cum_row, 0.0)), 0.0)
            low = split(jnp.where(strictly, beta_col * gram * mask, 0.0))
            grow = jnp.exp(cum_col)
            vf = v_all[span, h * dim : (h + 1) * dim].astype(f32)
            items.append(dict(
                c=c, h=h, low=low,
                x=eye - (low[0] * masks[0]).astype(f32) - (low[1] * masks[0]).astype(f32),
                rhs=split(jnp.concatenate([beta_col * vf, (beta_col * grow) * kf], axis=1)),
                scores=(qk * mask),
                qd=qf * grow,
                kd=k_turn * jnp.exp(last - cum_row),
                keep=jnp.exp(last),
            ))
    for mask in masks[1:]:
        for it in items:
            x = split(it["x"])
            part = dot3(x, (it["low"][0] * mask, it["low"][1] * mask))
            it["x"] = it["x"] - dot3(split(part), x)
    for it in items:
        it["uw"] = dot3(split(it["x"]), it["rhs"])
    states = [None] * ratio
    for it in items:
        c, h = it["c"], it["h"]
        u, w = it["uw"][:, :dim], it["uw"][:, dim:]
        zero = jnp.zeros((size, dim), f32)
        if c == 0:
            new = jnp.concatenate([u, -w], axis=1)
            seen = jnp.concatenate([zero, it["qd"]], axis=1)
            kept = jnp.concatenate([jnp.zeros((dim, dim), f32), it["keep"] * eye], axis=1)
        else:
            both = split(jnp.concatenate([w, it["qd"]], axis=0))
            got = dot3(both, split(states[h]))
            new = jnp.concatenate([u, zero], axis=1) - got[:size]
            seen = got[size:]
            kept = it["keep"] * states[h]
        new = split(new)
        out = seen + dot3(split(it["scores"]), new)
        states[h] = kept + dot3(split(it["kd"]), new)
        span = pl.ds(c * size, size)
        out_ref[span, h * dim : (h + 1) * dim] = out[:, :dim]
        eff_ref[span, h * dim : (h + 1) * dim] = out[:, dim:]
    for h in range(ratio):
        state_ref[h] = states[h][:, :dim]
        prod_ref[h] = states[h][:, dim:]


def final_kernel(out_ref, eff_ref, inc_ref, gate_ref, gain_ref, res_ref):
    core = out_ref[...] + dot3(split(eff_ref[...]), split(inc_ref[0]))
    gate = gate_ref[...].astype(f32)
    normed = core * lax.rsqrt(jnp.mean(core * core, axis=-1, keepdims=True) + norm_eps)
    res_ref[...] = (normed * gain_ref[...] * silu(gate)).astype(bf16)


def shifted(value, axis, steps):
    count = lax.axis_size(axis)
    first, last = (max(0, -steps), min(count, count - steps))
    return lax.ppermute(value, axis, [(source, source + steps) for source in range(first, last)])


def body(
    query_in, key_in, value_in, query_taps, key_taps, value_taps,
    log_decay, beta_logit, gate_in, norm_gain,
):
    dim = norm_gain.shape[0]
    length = query_in.shape[0]
    value_heads = log_decay.shape[0]
    key_heads = query_in.shape[1] // dim
    ratio = value_heads // key_heads
    taps = query_taps.shape[0]
    tails = shifted(
        jnp.concatenate([query_in[-PAD:], key_in[-PAD:], value_in[-PAD:]], axis=1), "ctx", 1
    )
    wide = ratio * dim

    def block(rows, width, first=0):
        return pl.BlockSpec((rows, width), lambda i: (0, first + i))

    rates = pl.BlockSpec((1, ratio, length), lambda i: (i, 0, 0))
    mats = pl.BlockSpec((ratio, dim, dim), lambda i: (i, 0, 0))
    mat_shape = jax.ShapeDtypeStruct((value_heads, dim, dim), f32)
    wide_shape = jax.ShapeDtypeStruct((length, value_heads * dim), f32)
    local_out, effect, local_state, product = pl.pallas_call(
        local_kernel,
        grid=(key_heads,),
        in_specs=[
            block(length, dim), block(length, dim), block(length, wide),
            block(PAD, dim), block(PAD, dim, key_heads), block(PAD, wide, 2 * key_heads // ratio),
            block(taps, dim), block(taps, dim), block(taps, wide),
            rates, rates,
        ],
        out_specs=[block(length, wide), block(length, wide), mats, mats],
        out_shape=[wide_shape, wide_shape, mat_shape, mat_shape],
        scratch_shapes=[
            pltpu.VMEM((length + PAD, dim), f32),
            pltpu.VMEM((length + PAD, wide), f32),
        ],
        compiler_params=pltpu.CompilerParams(vmem_limit_bytes=48 * 1024 * 1024),
        name="local",
    )(
        query_in, key_in, value_in, tails, tails, tails, query_taps, key_taps, value_taps,
        log_decay.reshape(key_heads, ratio, length), beta_logit.reshape(key_heads, ratio, length),
    )

    def chain_turn(turn, incoming):
        moved = jnp.einsum("hij,hjk->hik", product, incoming, precision=highest)
        return shifted(moved + local_state, "ctx", 1)

    zero_state = jnp.zeros((value_heads, dim, dim), f32)
    incoming = lax.fori_loop(0, lax.axis_size("ctx") - 1, chain_turn, zero_state)

    normed = pl.pallas_call(
        final_kernel,
        grid=(value_heads,),
        in_specs=[
            block(length, dim), block(length, dim),
            pl.BlockSpec((1, dim, dim), lambda i: (i, 0, 0)),
            block(length, dim),
            pl.BlockSpec((1, dim), lambda i: (0, 0)),
        ],
        out_specs=block(length, dim),
        out_shape=jax.ShapeDtypeStruct((length, value_heads * dim), bf16),
        compiler_params=pltpu.CompilerParams(vmem_limit_bytes=48 * 1024 * 1024),
        name="final",
    )(local_out, effect, incoming, gate_in, norm_gain.reshape(1, dim))
    return lax.all_to_all(normed, "head", split_axis=0, concat_axis=1, tiled=True)


def solution(mesh):
    in_specs = (
        P("ctx", "head"), P("ctx", "head"), P("ctx", "head"),
        P(None, "head"), P(None, "head"), P(None, "head"),
        P("head", "ctx"), P("head", "ctx"), P("ctx", "head"), P(),
    )
    out_specs = P(("ctx", "head"), None)
    return jax.shard_map(body, mesh=mesh, in_specs=in_specs, out_specs=out_specs, check_vma=False)
```

time: 612 us -> 182 us (0.30)
  the two profiles are of different devices: /device:TPU:27 before, /device:TPU:16 now
where the time goes in v1:
time: 182 us; the launch traced here: 181 us
  waiting for transfers between devices  81.9 us (45%)
  Pallas kernels  33.7 us (19%)
  matrix products  19.7 us (11%)
  starting transfers between devices  17.3 us (10%)
  blocking collectives  17.1 us (9%)
  local copies, waits for them, and re-layouts  11 us (6%)
    ppermute x8, waiting for transfers between devices, shifted(): lax.ppermute(value, axis, [(source, source + steps) for source in range(f...  81.9 us
    pallas_call x1, Pallas kernels, body(): pl.pallas_call(local_kernel, grid=(key_heads,), in_specs=[block(length, d...  27.6 us
    dot_general x7, matrix products, chain_turn(): moved = jnp.einsum('hij,hjk->hik', product, incoming, precision=highest)  19.7 us
    ppermute x8, starting transfers between devices, shifted(): lax.ppermute(value, axis, [(source, source + steps) for source in range(f...  17.3 us
    all_to_all x1, blocking collectives, body(): lax.all_to_all(normed, 'head', split_axis=0, concat_axis=1, tiled=True)  17.1 us
    pallas_call x1, Pallas kernels, body(): pl.pallas_call(final_kernel, grid=(value_heads,), in_specs=[block(length,...  6.05 us
    unnamed x16, local copies, waits for them, and re-layouts  5.42 us
  transfers between devices with their start and end apart: 8, of which 8 were waited for; matrix products, arithmetic and copies ran while one was open for 1% of the time, Pallas kernels for 0%

profile of v1, /device:TPU:16, one launch (start us, length us, event | category | flops | bytes accessed | tf_op | source)
XLA Modules:
  0.0 180.8 jit_solution(18079079246024294310)
XLA Ops:
  0.0 0.7 slice.9
  0.7 0.7 slice.10
  1.4 0.8 slice.11
  2.2 3.4 %collective-permute-start.1 = (bf16[16,2048]{1,0:T(8,128)(2,1)S(1)}, bf16[16,2048]{1,0:T(8,128)(2,1)S(1)}, u32[]{:S(2)}, u32[]{:S(2)}) collective-permute-start(bf16[16,2048]{1,0:T(8,128)(2,1)S(1)} %pad_maximum_fusion), channel_id=1, source_target_pairs={{0,4},{4,8},{8,12},{12,16},{16,20},{20,24},{24,28},{1,5},{5,9},{9,... | collective-permute-start | bytes 196616 | tf_op jit(solution)/shard_map/ppermute | solution.py:155
  5.6 0.7 reshape.12.ld_ref
  6.3 0.7 reshape.13.bl_ref
  7.1 2.2 %collective-permute-done.1.qt_ref.kt_ref.vt_ref = bf16[16,2048]{1,0:T(8,128)(2,1)S(1)} collective-permute-done((bf16[16,2048]{1,0:T(8,128)(2,1)S(1)}, bf16[16,2048]{1,0:T(8,128)(2,1)S(1)}, u32[]{:S(2)}, u32[]{:S(2)}) %collective-permute-start.1) | collective-permute-done | bytes 65568 | tf_op jit(solution)/shard_map/ppermute | solution.py:155
  9.3 0.0 copy-start
  9.3 1.2 copy-done
  10.5 0.0 copy-start.2
  10.5 1.0 copy-done.2
  11.5 0.0 copy-start.3
  11.5 1.0 copy-done.3
  12.6 0.0 copy-start.4
  12.6 0.7 copy-done.4
  13.3 0.0 copy-start.5
  13.3 0.7 copy-done.5
  14.0 0.0 copy-start.6
  14.0 0.7 copy-done.6
  14.7 27.6 %local.1 = (f32[512,1024]{1,0:T(8,128)S(1)}, f32[512,1024]{1,0:T(8,128)}, f32[8,128,128]{2,1,0:T(8,128)}, f32[8,128,128]{2,1,0:T(8,128)}) custom-call(bf16[512,512]{1,0:T(8,128)(2,1)S(1)} %copy-done.2, bf16[512,512]{1,0:T(8,128)(2,1)S(1)} %copy-done.3, bf16[512,1024]{1,0:T(8,128)(2,1)S(1)} %copy-done, ...), custom_call_target="tpu_custom_call" | custom-call | tf_op jit(solution)/shard_map/local/pallas_call | solution.py:180
  42.3 0.9 broadcast_in_dim.3
  43.1 0.0 copy-start.1
  43.1 0.0 copy-start.7
  43.1 113.4 %while.10 = (s32[]{:T(128)}, f32[8,128,128]{2,1,0:T(8,128)}, f32[8,128,128]{2,1,0:T(8,128)}, f32[8,128,128]{2,1,0:T(8,128)}, s32[]{:T(128)}) while((s32[]{:T(128)}, f32[8,128,128]{2,1,0:T(8,128)}, f32[8,128,128]{2,1,0:T(8,128)}, f32[8,128,128]{2,1,0:T(8,128)}, s32[]{:T(128)}) %tuple.18), condition=%wide.region_1.0_spmd, body=%wide.region_0.0_spmd.sunk | while | flops 201457664 | bytes 4194405 | solution.py:207
  43.1 2.9 %convolution_add_fusion.2 = f32[8,128,128]{2,1,0:T(8,128)} fusion(f32[8,128,128]{2,1,0:T(8,128)} %get-tuple-element.82, f32[8,128,128]{2,1,0:T(8,128)} %get-tuple-element.81, f32[8,128,128]{2,1,0:T(8,128)} %get-tuple-element.75), kind=kOutput, calls=%fused_computation.clone.1 | convolution fusion | flops 201457664 | bytes 2097152 | tf_op jit(solution)/shard_map/while/body/eval_jaxpr/hij,hjk->hik/dot_general | solution.py:203
  46.0 2.5 %collective-permute-start = (f32[8,128,128]{2,1,0:T(8,128)}, f32[8,128,128]{2,1,0:T(8,128)}, u32[]{:S(2)}, u32[]{:S(2)}) collective-permute-start(f32[8,128,128]{2,1,0:T(8,128)} %convolution_add_fusion.2), channel_id=1, source_target_pairs={{0,4},{4,8},{8,12},{12,16},{16,20},{20,24},{24,28},{1,5},{5,9},{9,... | collective-permute-start | bytes 1572872 | tf_op jit(solution)/shard_map/while/body/eval_jaxpr/ppermute | solution.py:155
  48.5 13.1 %collective-permute-done = f32[8,128,128]{2,1,0:T(8,128)} collective-permute-done((f32[8,128,128]{2,1,0:T(8,128)}, f32[8,128,128]{2,1,0:T(8,128)}, u32[]{:S(2)}, u32[]{:S(2)}) %collective-permute-start) | collective-permute-done | bytes 524320 | tf_op jit(solution)/shard_map/while/body/eval_jaxpr/ppermute | solution.py:155
  61.6 2.8 %convolution_add_fusion.2 = f32[8,128,128]{2,1,0:T(8,128)} fusion(f32[8,128,128]{2,1,0:T(8,128)} %get-tuple-element.82, f32[8,128,128]{2,1,0:T(8,128)} %get-tuple-element.81, f32[8,128,128]{2,1,0:T(8,128)} %get-tuple-element.75), kind=kOutput, calls=%fused_computation.clone.1 | convolution fusion | flops 201457664 | bytes 2097152 | tf_op jit(solution)/shard_map/while/body/eval_jaxpr/hij,hjk->hik/dot_general | solution.py:203
  64.5 1.9 %collective-permute-start = (f32[8,128,128]{2,1,0:T(8,128)}, f32[8,128,128]{2,1,0:T(8,128)}, u32[]{:S(2)}, u32[]{:S(2)}) collective-permute-start(f32[8,128,128]{2,1,0:T(8,128)} %convolution_add_fusion.2), channel_id=1, source_target_pairs={{0,4},{4,8},{8,12},{12,16},{16,20},{20,24},{24,28},{1,5},{5,9},{9,... | collective-permute-start | bytes 1572872 | tf_op jit(solution)/shard_map/while/body/eval_jaxpr/ppermute | solution.py:155
  66.4 12.8 %collective-permute-done = f32[8,128,128]{2,1,0:T(8,128)} collective-permute-done((f32[8,128,128]{2,1,0:T(8,128)}, f32[8,128,128]{2,1,0:T(8,128)}, u32[]{:S(2)}, u32[]{:S(2)}) %collective-permute-start) | collective-permute-done | bytes 524320 | tf_op jit(solution)/shard_map/while/body/eval_jaxpr/ppermute | solution.py:155
  79.1 2.8 %convolution_add_fusion.2 = f32[8,128,128]{2,1,0:T(8,128)} fusion(f32[8,128,128]{2,1,0:T(8,128)} %get-tuple-element.82, f32[8,128,128]{2,1,0:T(8,128)} %get-tuple-element.81, f32[8,128,128]{2,1,0:T(8,128)} %get-tuple-element.75), kind=kOutput, calls=%fused_computation.clone.1 | convolution fusion | flops 201457664 | bytes 2097152 | tf_op jit(solution)/shard_map/while/body/eval_jaxpr/hij,hjk->hik/dot_general | solution.py:203
  81.9 1.9 %collective-permute-start = (f32[8,128,128]{2,1,0:T(8,128)}, f32[8,128,128]{2,1,0:T(8,128)}, u32[]{:S(2)}, u32[]{:S(2)}) collective-permute-start(f32[8,128,128]{2,1,0:T(8,128)} %convolution_add_fusion.2), channel_id=1, source_target_pairs={{0,4},{4,8},{8,12},{12,16},{16,20},{20,24},{24,28},{1,5},{5,9},{9,... | collective-permute-start | bytes 1572872 | tf_op jit(solution)/shard_map/while/body/eval_jaxpr/ppermute | solution.py:155
  83.9 11.8 %collective-permute-done = f32[8,128,128]{2,1,0:T(8,128)} collective-permute-done((f32[8,128,128]{2,1,0:T(8,128)}, f32[8,128,128]{2,1,0:T(8,128)}, u32[]{:S(2)}, u32[]{:S(2)}) %collective-permute-start) | collective-permute-done | bytes 524320 | tf_op jit(solution)/shard_map/while/body/eval_jaxpr/ppermute | solution.py:155
  95.7 2.8 %convolution_add_fusion.2 = f32[8,128,128]{2,1,0:T(8,128)} fusion(f32[8,128,128]{2,1,0:T(8,128)} %get-tuple-element.82, f32[8,128,128]{2,1,0:T(8,128)} %get-tuple-element.81, f32[8,128,128]{2,1,0:T(8,128)} %get-tuple-element.75), kind=kOutput, calls=%fused_computation.clone.1 | convolution fusion | flops 201457664 | bytes 2097152 | tf_op jit(solution)/shard_map/while/body/eval_jaxpr/hij,hjk->hik/dot_general | solution.py:203
  98.5 1.9 %collective-permute-start = (f32[8,128,128]{2,1,0:T(8,128)}, f32[8,128,128]{2,1,0:T(8,128)}, u32[]{:S(2)}, u32[]{:S(2)}) collective-permute-start(f32[8,128,128]{2,1,0:T(8,128)} %convolution_add_fusion.2), channel_id=1, source_target_pairs={{0,4},{4,8},{8,12},{12,16},{16,20},{20,24},{24,28},{1,5},{5,9},{9,... | collective-permute-start | bytes 1572872 | tf_op jit(solution)/shard_map/while/body/eval_jaxpr/ppermute | solution.py:155
  100.4 10.9 %collective-permute-done = f32[8,128,128]{2,1,0:T(8,128)} collective-permute-done((f32[8,128,128]{2,1,0:T(8,128)}, f32[8,128,128]{2,1,0:T(8,128)}, u32[]{:S(2)}, u32[]{:S(2)}) %collective-permute-start) | collective-permute-done | bytes 524320 | tf_op jit(solution)/shard_map/while/body/eval_jaxpr/ppermute | solution.py:155
  111.4 2.8 %convolution_add_fusion.2 = f32[8,128,128]{2,1,0:T(8,128)} fusion(f32[8,128,128]{2,1,0:T(8,128)} %get-tuple-element.82, f32[8,128,128]{2,1,0:T(8,128)} %get-tuple-element.81, f32[8,128,128]{2,1,0:T(8,128)} %get-tuple-element.75), kind=kOutput, calls=%fused_computation.clone.1 | convolution fusion | flops 201457664 | bytes 2097152 | tf_op jit(solution)/shard_map/while/body/eval_jaxpr/hij,hjk->hik/dot_general | solution.py:203
  114.2 1.9 %collective-permute-start = (f32[8,128,128]{2,1,0:T(8,128)}, f32[8,128,128]{2,1,0:T(8,128)}, u32[]{:S(2)}, u32[]{:S(2)}) collective-permute-start(f32[8,128,128]{2,1,0:T(8,128)} %convolution_add_fusion.2), channel_id=1, source_target_pairs={{0,4},{4,8},{8,12},{12,16},{16,20},{20,24},{24,28},{1,5},{5,9},{9,... | collective-permute-start | bytes 1572872 | tf_op jit(solution)/shard_map/while/body/eval_jaxpr/ppermute | solution.py:155
  116.1 10.4 %collective-permute-done = f32[8,128,128]{2,1,0:T(8,128)} collective-permute-done((f32[8,128,128]{2,1,0:T(8,128)}, f32[8,128,128]{2,1,0:T(8,128)}, u32[]{:S(2)}, u32[]{:S(2)}) %collective-permute-start) | collective-permute-done | bytes 524320 | tf_op jit(solution)/shard_map/while/body/eval_jaxpr/ppermute | solution.py:155
  126.4 2.8 %convolution_add_fusion.2 = f32[8,128,128]{2,1,0:T(8,128)} fusion(f32[8,128,128]{2,1,0:T(8,128)} %get-tuple-element.82, f32[8,128,128]{2,1,0:T(8,128)} %get-tuple-element.81, f32[8,128,128]{2,1,0:T(8,128)} %get-tuple-element.75), kind=kOutput, calls=%fused_computation.clone.1 | convolution fusion | flops 201457664 | bytes 2097152 | tf_op jit(solution)/shard_map/while/body/eval_jaxpr/hij,hjk->hik/dot_general | solution.py:203
  129.2 1.9 %collective-permute-start = (f32[8,128,128]{2,1,0:T(8,128)}, f32[8,128,128]{2,1,0:T(8,128)}, u32[]{:S(2)}, u32[]{:S(2)}) collective-permute-start(f32[8,128,128]{2,1,0:T(8,128)} %convolution_add_fusion.2), channel_id=1, source_target_pairs={{0,4},{4,8},{8,12},{12,16},{16,20},{20,24},{24,28},{1,5},{5,9},{9,... | collective-permute-start | bytes 1572872 | tf_op jit(solution)/shard_map/while/body/eval_jaxpr/ppermute | solution.py:155
  131.2 10.4 %collective-permute-done = f32[8,128,128]{2,1,0:T(8,128)} collective-permute-done((f32[8,128,128]{2,1,0:T(8,128)}, f32[8,128,128]{2,1,0:T(8,128)}, u32[]{:S(2)}, u32[]{:S(2)}) %collective-permute-start) | collective-permute-done | bytes 524320 | tf_op jit(solution)/shard_map/while/body/eval_jaxpr/ppermute | solution.py:155
  141.5 2.8 %convolution_add_fusion.2 = f32[8,128,128]{2,1,0:T(8,128)} fusion(f32[8,128,128]{2,1,0:T(8,128)} %get-tuple-element.82, f32[8,128,128]{2,1,0:T(8,128)} %get-tuple-element.81, f32[8,128,128]{2,1,0:T(8,128)} %get-tuple-element.75), kind=kOutput, calls=%fused_computation.clone.1 | convolution fusion | flops 201457664 | bytes 2097152 | tf_op jit(solution)/shard_map/while/body/eval_jaxpr/hij,hjk->hik/dot_general | solution.py:203
  144.3 1.9 %collective-permute-start = (f32[8,128,128]{2,1,0:T(8,128)}, f32[8,128,128]{2,1,0:T(8,128)}, u32[]{:S(2)}, u32[]{:S(2)}) collective-permute-start(f32[8,128,128]{2,1,0:T(8,128)} %convolution_add_fusion.2), channel_id=1, source_target_pairs={{0,4},{4,8},{8,12},{12,16},{16,20},{20,24},{24,28},{1,5},{5,9},{9,... | collective-permute-start | bytes 1572872 | tf_op jit(solution)/shard_map/while/body/eval_jaxpr/ppermute | solution.py:155
  146.2 10.4 %collective-permute-done = f32[8,128,128]{2,1,0:T(8,128)} collective-permute-done((f32[8,128,128]{2,1,0:T(8,128)}, f32[8,128,128]{2,1,0:T(8,128)}, u32[]{:S(2)}, u32[]{:S(2)}) %collective-permute-start) | collective-permute-done | bytes 524320 | tf_op jit(solution)/shard_map/while/body/eval_jaxpr/ppermute | solution.py:155
  156.6 0.0 copy-done.1
  156.6 0.0 copy-done.7
  156.6 6.1 %final.1 = bf16[512,1024]{1,0:T(8,128)(2,1)S(1)} custom-call(f32[512,1024]{1,0:T(8,128)S(1)} %get-tuple-element.31.out_ref, f32[512,1024]{1,0:T(8,128)} %get-tuple-element.32.eff_ref, f32[8,128,128]{2,1,0:T(8,128)} %get-tuple-element.35.inc_ref, bf16[512,1024]{1,0:T(8,128)(2,1)S(1)} %copy-done.1, f32[1,128]{1,0:T(1,128)S(1)} %bitcast.12), custom_call_target="tpu_custom_call" | custom-call | tf_op jit(solution)/shard_map/final/pallas_call | solution.py:209
  162.7 17.1 %all_to_all.19 = bf16[4,128,1024]{2,1,0:T(8,128)(2,1)S(1)} all-to-all(bf16[4,128,1024]{2,1,0:T(8,128)(2,1)S(1)} %bitcast.11), channel_id=1, replica_groups=mesh['ctx'=8,'head'=4] {'head'}, dimensions={0} | all-to-all | bytes 2097152 | tf_op jit(solution)/shard_map/all_to_all | solution.py:223
  179.7 1.1 copy.12
  (1 shorter events, 0.0 us)
Async XLA Ops:
  2.2 7.1 %collective-permute-start.1 = (bf16[16,2048]{1,0:T(8,128)(2,1)S(1)}, bf16[16,2048]{1,0:T(8,128)(2,1)S(1)}, u32[]{:S(2)}, u32[]{:S(2)}) collective-permute-start(bf16[16,2048]{1,0:T(8,128)(2,1)S(1)} %pad_maximum_fusion), channel_id=1, source_target_pairs={{0,4},{4,8},{8,12},{12,16},{16,20},{20,24},{24,28},{1,5},{5,9},{9,... | collective-permute-start | bytes 196616 | tf_op jit(solution)/shard_map/ppermute | solution.py:155
  9.3 1.2 copy-start
  10.5 1.0 copy-start.2
  11.5 1.0 copy-start.3
  12.6 0.7 copy-start.4
  13.3 0.7 copy-start.5
  14.0 0.7 copy-start.6
  43.1 113.5 %copy-start.1 = (bf16[512,1024]{1,0:T(8,128)(2,1)S(1)}, bf16[512,1024]{1,0:T(8,128)(2,1)}, u32[]{:S(2)}) copy-start(bf16[512,1024]{1,0:T(8,128)(2,1)} %gate_ref.1) | copy-start | bytes 3145732
  43.1 113.5 %copy-start.7 = (f32[128]{0:T(128)S(1)}, f32[128]{0:T(128)}, u32[]{:S(2)}) copy-start(f32[128]{0:T(128)} %param.21) | copy-start | bytes 1540
  46.0 15.6 %collective-permute-start = (f32[8,128,128]{2,1,0:T(8,128)}, f32[8,128,128]{2,1,0:T(8,128)}, u32[]{:S(2)}, u32[]{:S(2)}) collective-permute-start(f32[8,128,128]{2,1,0:T(8,128)} %convolution_add_fusion.2), channel_id=1, source_target_pairs={{0,4},{4,8},{8,12},{12,16},{16,20},{20,24},{24,28},{1,5},{5,9},{9,... | collective-permute-start | bytes 1572872 | tf_op jit(solution)/shard_map/while/body/eval_jaxpr/ppermute | solution.py:155
  64.5 14.7 %collective-permute-start = (f32[8,128,128]{2,1,0:T(8,128)}, f32[8,128,128]{2,1,0:T(8,128)}, u32[]{:S(2)}, u32[]{:S(2)}) collective-permute-start(f32[8,128,128]{2,1,0:T(8,128)} %convolution_add_fusion.2), channel_id=1, source_target_pairs={{0,4},{4,8},{8,12},{12,16},{16,20},{20,24},{24,28},{1,5},{5,9},{9,... | collective-permute-start | bytes 1572872 | tf_op jit(solution)/shard_map/while/body/eval_jaxpr/ppermute | solution.py:155
  81.9 13.8 %collective-permute-start = (f32[8,128,128]{2,1,0:T(8,128)}, f32[8,128,128]{2,1,0:T(8,128)}, u32[]{:S(2)}, u32[]{:S(2)}) collective-permute-start(f32[8,128,128]{2,1,0:T(8,128)} %convolution_add_fusion.2), channel_id=1, source_target_pairs={{0,4},{4,8},{8,12},{12,16},{16,20},{20,24},{24,28},{1,5},{5,9},{9,... | collective-permute-start | bytes 1572872 | tf_op jit(solution)/shard_map/while/body/eval_jaxpr/ppermute | solution.py:155
  98.5 12.8 %collective-permute-start = (f32[8,128,128]{2,1,0:T(8,128)}, f32[8,128,128]{2,1,0:T(8,128)}, u32[]{:S(2)}, u32[]{:S(2)}) collective-permute-start(f32[8,128,128]{2,1,0:T(8,128)} %convolution_add_fusion.2), channel_id=1, source_target_pairs={{0,4},{4,8},{8,12},{12,16},{16,20},{20,24},{24,28},{1,5},{5,9},{9,... | collective-permute-start | bytes 1572872 | tf_op jit(solution)/shard_map/while/body/eval_jaxpr/ppermute | solution.py:155
  114.2 12.3 %collective-permute-start = (f32[8,128,128]{2,1,0:T(8,128)}, f32[8,128,128]{2,1,0:T(8,128)}, u32[]{:S(2)}, u32[]{:S(2)}) collective-permute-start(f32[8,128,128]{2,1,0:T(8,128)} %convolution_add_fusion.2), channel_id=1, source_target_pairs={{0,4},{4,8},{8,12},{12,16},{16,20},{20,24},{24,28},{1,5},{5,9},{9,... | collective-permute-start | bytes 1572872 | tf_op jit(solution)/shard_map/while/body/eval_jaxpr/ppermute | solution.py:155
  129.2 12.3 %collective-permute-start = (f32[8,128,128]{2,1,0:T(8,128)}, f32[8,128,128]{2,1,0:T(8,128)}, u32[]{:S(2)}, u32[]{:S(2)}) collective-permute-start(f32[8,128,128]{2,1,0:T(8,128)} %convolution_add_fusion.2), channel_id=1, source_target_pairs={{0,4},{4,8},{8,12},{12,16},{16,20},{20,24},{24,28},{1,5},{5,9},{9,... | collective-permute-start | bytes 1572872 | tf_op jit(solution)/shard_map/while/body/eval_jaxpr/ppermute | solution.py:155
  144.3 12.3 %collective-permute-start = (f32[8,128,128]{2,1,0:T(8,128)}, f32[8,128,128]{2,1,0:T(8,128)}, u32[]{:S(2)}, u32[]{:S(2)}) collective-permute-start(f32[8,128,128]{2,1,0:T(8,128)} %convolution_add_fusion.2), channel_id=1, source_target_pairs={{0,4},{4,8},{8,12},{12,16},{16,20},{20,24},{24,28},{1,5},{5,9},{9,... | collective-permute-start | bytes 1572872 | tf_op jit(solution)/shard_map/while/body/eval_jaxpr/ppermute | solution.py:155

commit v2 on v1

--- a/solution.py
+++ b/solution.py
@@ -111,9 +111,13 @@
             ))
     for mask in masks[1:]:
         for it in items:
-            x = split(it["x"])
-            part = dot3(x, (it["low"][0] * mask, it["low"][1] * mask))
-            it["x"] = it["x"] - dot3(split(part), x)
+            x = it["x"].astype(bf16)
+            part = dot1(x, it["low"][0] * mask)
+            it["x"] = it["x"] - dot1(part.astype(bf16), x)
+    for it in items:
+        x = split(it["x"])
+        rest = (eye - it["x"]) - dot3(it["low"], x)
+        it["x"] = it["x"] + dot1(x[0], rest.astype(bf16))
     for it in items:
         it["uw"] = dot3(split(it["x"]), it["rhs"])
     states = [None] * ratio
@@ -132,7 +136,7 @@
             seen = got[size:]
             kept = it["keep"] * states[h]
         new = split(new)
-        out = seen + dot3(split(it["scores"]), new)
+        out = seen + dot1(it["scores"].astype(bf16), new[0])
         states[h] = kept + dot3(split(it["kd"]), new)
         span = pl.ds(c * size, size)
         out_ref[span, h * dim : (h + 1) * dim] = out[:, :dim]
@@ -142,11 +146,82 @@
         prod_ref[h] = states[h][:, dim:]
 
 
-def final_kernel(out_ref, eff_ref, inc_ref, gate_ref, gain_ref, res_ref):
-    core = out_ref[...] + dot3(split(eff_ref[...]), split(inc_ref[0]))
-    gate = gate_ref[...].astype(f32)
-    normed = core * lax.rsqrt(jnp.mean(core * core, axis=-1, keepdims=True) + norm_eps)
-    res_ref[...] = (normed * gain_ref[...] * silu(gate)).astype(bf16)
+def carry_kernel(
+    ring, peers, out_ref, eff_ref, state_ref, prod_ref, gate_ref, gain_ref, res_ref,
+    incoming, outgoing, stage, ring_send, ring_recv, peer_send, peer_recv,
+):
+    heads, dim, _ = state_ref.shape
+    rows = res_ref.shape[0]
+    me = lax.axis_index("ctx")
+    mine = lax.axis_index("head")
+    after, before = lax.rem(me + 1, ring), lax.rem(me + ring - 1, ring)
+    partners = [lax.rem(mine + d, peers) for d in range(1, peers)]
+    barrier = pltpu.get_barrier_semaphore()
+    for other in (after, before):
+        pl.semaphore_signal(
+            barrier, inc=1, device_id=(other, mine), device_id_type=pl.DeviceIdType.MESH
+        )
+    for other in partners:
+        pl.semaphore_signal(
+            barrier, inc=1, device_id=(me, other), device_id_type=pl.DeviceIdType.MESH
+        )
+    pl.semaphore_wait(barrier, 2 + len(partners))
+
+    def ring_copy(h):
+        return pltpu.make_async_remote_copy(
+            src_ref=outgoing.at[h], dst_ref=incoming.at[h],
+            send_sem=ring_send.at[h], recv_sem=ring_recv.at[h],
+            device_id=(after, mine), device_id_type=pl.DeviceIdType.MESH,
+        )
+
+    def peer_copy(h, d, other):
+        start = pl.multiple_of((mine * heads + h) * dim, dim)
+        return pltpu.make_async_remote_copy(
+            src_ref=stage.at[h, pl.ds(pl.multiple_of(other * rows, rows), rows), :],
+            dst_ref=res_ref.at[:, pl.ds(start, dim)],
+            send_sem=peer_send.at[h, d], recv_sem=peer_recv.at[h, d],
+            device_id=(me, other), device_id_type=pl.DeviceIdType.MESH,
+        )
+
+    @pl.when(me == 0)
+    def _():
+        incoming[...] = jnp.zeros_like(incoming)
+
+    def step(h, carry):
+        @pl.when(me > 0)
+        def _():
+            ring_copy(h).wait_recv()
+
+        state = split(incoming[h])
+
+        @pl.when(me < ring - 1)
+        def _():
+            outgoing[h] = state_ref[h] + dot3(split(prod_ref[h]), state)
+            ring_copy(h).start()
+
+        span = pl.ds(pl.multiple_of(h * dim, dim), dim)
+        core = out_ref[:, span] + dot1(eff_ref[:, span].astype(bf16), state[0])
+        gate = gate_ref[:, span].astype(f32)
+        normed = core * lax.rsqrt(jnp.mean(core * core, axis=-1, keepdims=True) + norm_eps)
+        stage[h] = (normed * gain_ref[...] * silu(gate)).astype(bf16)
+        for d, other in enumerate(partners):
+            peer_copy(h, d, other).start()
+        start = pl.multiple_of((mine * heads + h) * dim, dim)
+        res_ref[:, pl.ds(start, dim)] = stage[h, pl.ds(pl.multiple_of(mine * rows, rows), rows), :]
+        return carry
+
+    lax.fori_loop(0, heads, step, 0)
+
+    def drain(h, carry):
+        @pl.when(me < ring - 1)
+        def _():
+            ring_copy(h).wait_send()
+
+        for d, other in enumerate(partners):
+            peer_copy(h, d, other).wait()
+        return carry
+
+    lax.fori_loop(0, heads, drain, 0)
 
 
 def shifted(value, axis, steps):
@@ -199,28 +274,27 @@
         log_decay.reshape(key_heads, ratio, length), beta_logit.reshape(key_heads, ratio, length),
     )
 
-    def chain_turn(turn, incoming):
-        moved = jnp.einsum("hij,hjk->hik", product, incoming, precision=highest)
-        return shifted(moved + local_state, "ctx", 1)
-
-    zero_state = jnp.zeros((value_heads, dim, dim), f32)
-    incoming = lax.fori_loop(0, lax.axis_size("ctx") - 1, chain_turn, zero_state)
-
-    normed = pl.pallas_call(
-        final_kernel,
-        grid=(value_heads,),
-        in_specs=[
-            block(length, dim), block(length, dim),
-            pl.BlockSpec((1, dim, dim), lambda i: (i, 0, 0)),
-            block(length, dim),
-            pl.BlockSpec((1, dim), lambda i: (0, 0)),
+    ring, peers = lax.axis_size("ctx"), lax.axis_size("head")
+    whole = pl.BlockSpec(memory_space=pltpu.VMEM)
+    return pl.pallas_call(
+        functools.partial(carry_kernel, ring, peers),
+        in_specs=[whole] * 6,
+        out_specs=whole,
+        out_shape=jax.ShapeDtypeStruct((length // peers, peers * value_heads * dim), bf16),
+        scratch_shapes=[
+            pltpu.VMEM((value_heads, dim, dim), f32),
+            pltpu.VMEM((value_heads, dim, dim), f32),
+            pltpu.VMEM((value_heads, length, dim), bf16),
+            pltpu.SemaphoreType.DMA((value_heads,)),
+            pltpu.SemaphoreType.DMA((value_heads,)),
+            pltpu.SemaphoreType.DMA((value_heads, peers - 1)),
+            pltpu.SemaphoreType.DMA((value_heads, peers - 1)),
         ],
-        out_specs=block(length, dim),
-        out_shape=jax.ShapeDtypeStruct((length, value_heads * dim), bf16),
-        compiler_params=pltpu.CompilerParams(vmem_limit_bytes=48 * 1024 * 1024),
-        name="final",
-    )(local_out, effect, incoming, gate_in, norm_gain.reshape(1, dim))
-    return lax.all_to_all(normed, "head", split_axis=0, concat_axis=1, tiled=True)
+        compiler_params=pltpu.CompilerParams(
+            collective_id=0, has_side_effects=True, vmem_limit_bytes=40 * 1024 * 1024
+        ),
+        name="carry",
+    )(local_out, effect, local_state, product, gate_in, norm_gain.reshape(1, dim))
 
 
 def solution(mesh):

time: 182 us -> 86.2 us (0.47)
  the two profiles are of different devices: /device:TPU:16 before, /device:TPU:27 now
where the time goes in v2:
time: 86.2 us; the launch traced here: 85.5 us
  Pallas kernels  70.3 us (82%)
  local copies, waits for them, and re-layouts  11.7 us (14%)
  waiting for transfers between devices  2.24 us (3%)
  starting transfers between devices  1.29 us (1%)
    pallas_call x1, Pallas kernels, body(): pl.pallas_call(functools.partial(carry_kernel, ring, peers), in_specs=[wh...  42.5 us
    pallas_call x1, Pallas kernels, body(): pl.pallas_call(local_kernel, grid=(key_heads,), in_specs=[block(length, d...  27.8 us
    unnamed x19, local copies, waits for them, and re-layouts  7.99 us
    ppermute x1, waiting for transfers between devices, shifted(): lax.ppermute(value, axis, [(source, source + steps) for source in range(f...  2.24 us
  transfers between devices with their start and end apart: 1, of which 1 were waited for; matrix products, arithmetic and copies ran while one was open for 2% of the time, Pallas kernels for 0%

profile of v2, /device:TPU:27, one launch (start us, length us, event | category | flops | bytes accessed | tf_op | source)
XLA Modules:
  0.0 85.5 jit_solution(1281060663692412309)
XLA Ops:
  0.0 0.0 copy-start.8
  0.0 0.7 slice.9
  0.7 0.7 slice.10
  1.5 0.8 slice.11
  2.2 1.3 %collective-permute-start = (bf16[16,2048]{1,0:T(8,128)(2,1)S(1)}, bf16[16,2048]{1,0:T(8,128)(2,1)S(1)}, u32[]{:S(2)}, u32[]{:S(2)}) collective-permute-start(bf16[16,2048]{1,0:T(8,128)(2,1)S(1)} %pad_maximum_fusion), channel_id=1, source_target_pairs={{0,4},{4,8},{8,12},{12,16},{16,20},{20,24},{24,28},{1,5},{5,9},{9,... | collective-permute-start | bytes 196616 | tf_op jit(solution)/shard_map/ppermute | solution.py:230
  3.5 0.7 reshape.9.ld_ref
  4.2 0.7 reshape.10.bl_ref
  5.0 2.2 %collective-permute-done.qt_ref.kt_ref.vt_ref = bf16[16,2048]{1,0:T(8,128)(2,1)S(1)} collective-permute-done((bf16[16,2048]{1,0:T(8,128)(2,1)S(1)}, bf16[16,2048]{1,0:T(8,128)(2,1)S(1)}, u32[]{:S(2)}, u32[]{:S(2)}) %collective-permute-start) | collective-permute-done | bytes 65568 | tf_op jit(solution)/shard_map/ppermute | solution.py:230
  7.2 0.0 copy-start.1
  7.2 1.2 %copy-done.1 = bf16[512,1024]{1,0:T(8,128)(2,1)S(1)} copy-done((bf16[512,1024]{1,0:T(8,128)(2,1)S(1)}, bf16[512,1024]{1,0:T(8,128)(2,1)}, u32[]{:S(2)}) %copy-start.1) | copy-done | bytes 1048600
  8.5 0.0 copy-start.3
  8.5 1.0 %copy-done.3 = bf16[512,512]{1,0:T(8,128)(2,1)S(1)} copy-done((bf16[512,512]{1,0:T(8,128)(2,1)S(1)}, bf16[512,512]{1,0:T(8,128)(2,1)}, u32[]{:S(2)}) %copy-start.3) | copy-done | bytes 524312
  9.5 0.0 copy-start.4
  9.5 1.0 %copy-done.4 = bf16[512,512]{1,0:T(8,128)(2,1)S(1)} copy-done((bf16[512,512]{1,0:T(8,128)(2,1)S(1)}, bf16[512,512]{1,0:T(8,128)(2,1)}, u32[]{:S(2)}) %copy-start.4) | copy-done | bytes 524312
  10.5 0.0 copy-start.5
  10.5 0.7 copy-done.5
  11.3 0.0 copy-start.6
  11.3 0.7 copy-done.6
  12.0 0.0 copy-start.7
  12.0 0.7 copy-done.7
  12.6 0.0 copy-start.2
  12.7 27.8 %local.1 = (f32[512,1024]{1,0:T(8,128)S(1)}, f32[512,1024]{1,0:T(8,128)}, f32[8,128,128]{2,1,0:T(8,128)S(1)}, f32[8,128,128]{2,1,0:T(8,128)S(1)}) custom-call(bf16[512,512]{1,0:T(8,128)(2,1)S(1)} %copy-done.3, bf16[512,512]{1,0:T(8,128)(2,1)S(1)} %copy-done.4, bf16[512,1024]{1,0:T(8,128)(2,1)S(1)} %copy-done.1, ...), custom_call_target="tpu_custom_call" | custom-call | tf_op jit(solution)/shard_map/local/pallas_call | solution.py:255
  40.5 0.0 copy-done.8
  40.5 0.0 copy-done.2
  40.5 0.0 copy-start
  40.5 1.6 %copy-done = f32[512,1024]{1,0:T(8,128)S(1)} copy-done((f32[512,1024]{1,0:T(8,128)S(1)}, f32[512,1024]{1,0:T(8,128)}, u32[]{:S(2)}) %copy-start) | copy-done | bytes 2097176
  42.1 42.5 %carry.1 = bf16[128,4096]{1,0:T(8,128)(2,1)S(1)} custom-call(f32[512,1024]{1,0:T(8,128)S(1)} %get-tuple-element.9.out_ref, f32[512,1024]{1,0:T(8,128)S(1)} %copy-done, f32[8,128,128]{2,1,0:T(8,128)S(1)} %get-tuple-element.11.state_ref, f32[8,128,128]{2,1,0:T(8,128)S(1)} %get-tuple-element.12.prod_ref, bf16[512,1024]{1,0:T(8,128)(2,1)S(1)} %copy-done.2, ...), custom_call_target="tpu_custom_call" | custom-call | tf_op jit(solution)/shard_map/carry/pallas_call | solution.py:279
  84.5 1.0 %copy.12 = bf16[128,4096]{1,0:T(8,128)(2,1)} copy(bf16[128,4096]{1,0:T(8,128)(2,1)S(1)} %carry.1) | data formatting | bytes 2097152
  (1 shorter events, 0.0 us)
Async XLA Ops:
  0.0 40.5 %copy-start.8 = (f32[128]{0:T(128)S(1)}, f32[128]{0:T(128)}, u32[]{:S(2)}) copy-start(f32[128]{0:T(128)} %param.19) | copy-start | bytes 1540
  2.2 5.0 %collective-permute-start = (bf16[16,2048]{1,0:T(8,128)(2,1)S(1)}, bf16[16,2048]{1,0:T(8,128)(2,1)S(1)}, u32[]{:S(2)}, u32[]{:S(2)}) collective-permute-start(bf16[16,2048]{1,0:T(8,128)(2,1)S(1)} %pad_maximum_fusion), channel_id=1, source_target_pairs={{0,4},{4,8},{8,12},{12,16},{16,20},{20,24},{24,28},{1,5},{5,9},{9,... | collective-permute-start | bytes 196616 | tf_op jit(solution)/shard_map/ppermute | solution.py:230
  7.2 1.2 %copy-start.1 = (bf16[512,1024]{1,0:T(8,128)(2,1)S(1)}, bf16[512,1024]{1,0:T(8,128)(2,1)}, u32[]{:S(2)}) copy-start(bf16[512,1024]{1,0:T(8,128)(2,1)} %v_ref.1) | copy-start | bytes 3145732
  8.5 1.0 %copy-start.3 = (bf16[512,512]{1,0:T(8,128)(2,1)S(1)}, bf16[512,512]{1,0:T(8,128)(2,1)}, u32[]{:S(2)}) copy-start(bf16[512,512]{1,0:T(8,128)(2,1)} %q_ref.1) | copy-start | bytes 1572868
  9.5 1.0 %copy-start.4 = (bf16[512,512]{1,0:T(8,128)(2,1)S(1)}, bf16[512,512]{1,0:T(8,128)(2,1)}, u32[]{:S(2)}) copy-start(bf16[512,512]{1,0:T(8,128)(2,1)} %k_ref.1) | copy-start | bytes 1572868
  10.5 0.7 copy-start.5
  11.3 0.7 copy-start.6
  12.0 0.7 copy-start.7
  12.6 27.8 %copy-start.2 = (bf16[512,1024]{1,0:T(8,128)(2,1)S(1)}, bf16[512,1024]{1,0:T(8,128)(2,1)}, u32[]{:S(2)}) copy-start(bf16[512,1024]{1,0:T(8,128)(2,1)} %gate_ref.1) | copy-start | bytes 3145732
  40.5 1.6 %copy-start = (f32[512,1024]{1,0:T(8,128)S(1)}, f32[512,1024]{1,0:T(8,128)}, u32[]{:S(2)}) copy-start(f32[512,1024]{1,0:T(8,128)} %get-tuple-element.10.eff_ref) | copy-start | bytes 6291460

commit v3 on v2

--- a/solution.py
+++ b/solution.py
@@ -66,14 +66,20 @@
     strictly = cols < rows
     eye = jnp.where(cols == rows, 1.0, 0.0).astype(f32)
     upper = jnp.where(rows <= cols, 1.0, 0.0).astype(f32)
+    apart = rows ^ cols
     masks = []
     width = 1
     while width < size:
-        pick = (rows // (2 * width) == cols // (2 * width)) & (rows // width != cols // width)
-        masks.append(jnp.where(pick & strictly, 1.0, 0.0).astype(bf16))
+        pick = (apart >= width) & (apart < 2 * width)
+        masks.append(jnp.where(pick, 1.0, 0.0).astype(bf16))
         width *= 2
 
-    beta_all = 1.0 / (1.0 + jnp.exp(-bl_ref[0]))
+    def rate_rows(ref):
+        first = pl.program_id(0) * ratio
+        return jnp.concatenate([ref[pl.ds(first + h, 1), :] for h in range(ratio)], axis=0)
+
+    beta_all = 1.0 / (1.0 + jnp.exp(-rate_rows(bl_ref)))
+    decay_all = rate_rows(ld_ref)
     items = []
     for c in range(length // size):
         span = slice(c * size, (c + 1) * size)
@@ -84,7 +90,7 @@
         gram = lax.dot_general(kc, kc, nt, preferred_element_type=f32)
         qk = lax.dot_general(qc, kc, nt, preferred_element_type=f32)
         cum = lax.dot_general(
-            ld_ref[0][:, span], upper, (((1,), (0,)), ((), ())),
+            decay_all[:, span], upper, (((1,), (0,)), ((), ())),
             precision=highest, preferred_element_type=f32,
         )
         stacked = jnp.concatenate(
@@ -148,7 +154,7 @@
 
 def carry_kernel(
     ring, peers, out_ref, eff_ref, state_ref, prod_ref, gate_ref, gain_ref, res_ref,
-    incoming, outgoing, stage, ring_send, ring_recv, peer_send, peer_recv,
+    incoming, outgoing, stage, factor, ring_send, ring_recv, peer_send, peer_recv,
 ):
     heads, dim, _ = state_ref.shape
     rows = res_ref.shape[0]
@@ -167,9 +173,9 @@
         )
     pl.semaphore_wait(barrier, 2 + len(partners))
 
-    def ring_copy(h):
+    def ring_copy(h, source):
         return pltpu.make_async_remote_copy(
-            src_ref=outgoing.at[h], dst_ref=incoming.at[h],
+            src_ref=source.at[h], dst_ref=incoming.at[h],
             send_sem=ring_send.at[h], recv_sem=ring_recv.at[h],
             device_id=(after, mine), device_id_type=pl.DeviceIdType.MESH,
         )
@@ -183,27 +189,40 @@
             device_id=(me, other), device_id_type=pl.DeviceIdType.MESH,
         )
 
+    def head_span(h):
+        return pl.ds(pl.multiple_of(h * dim, dim), dim)
+
     @pl.when(me == 0)
     def _():
+        def send(h, carry):
+            ring_copy(h, state_ref).start()
+            return carry
+
+        lax.fori_loop(0, heads, send, 0)
         incoming[...] = jnp.zeros_like(incoming)
+
+    def gates(h, carry):
+        factor[h] = gain_ref[...] * silu(gate_ref[:, head_span(h)].astype(f32))
+        return carry
+
+    lax.fori_loop(0, heads, gates, 0)
 
     def step(h, carry):
         @pl.when(me > 0)
         def _():
-            ring_copy(h).wait_recv()
+            ring_copy(h, outgoing).wait_recv()
 
         state = split(incoming[h])
 
-        @pl.when(me < ring - 1)
+        @pl.when((me > 0) & (me < ring - 1))
         def _():
             outgoing[h] = state_ref[h] + dot3(split(prod_ref[h]), state)
-            ring_copy(h).start()
-
-        span = pl.ds(pl.multiple_of(h * dim, dim), dim)
+            ring_copy(h, outgoing).start()
+
+        span = head_span(h)
         core = out_ref[:, span] + dot1(eff_ref[:, span].astype(bf16), state[0])
-        gate = gate_ref[:, span].astype(f32)
-        normed = core * lax.rsqrt(jnp.mean(core * core, axis=-1, keepdims=True) + norm_eps)
-        stage[h] = (normed * gain_ref[...] * silu(gate)).astype(bf16)
+        scale = lax.rsqrt(jnp.mean(core * core, axis=-1, keepdims=True) + norm_eps)
+        stage[h] = (core * scale * factor[h]).astype(bf16)
         for d, other in enumerate(partners):
             peer_copy(h, d, other).start()
         start = pl.multiple_of((mine * heads + h) * dim, dim)
@@ -215,7 +234,7 @@
     def drain(h, carry):
         @pl.when(me < ring - 1)
         def _():
-            ring_copy(h).wait_send()
+            ring_copy(h, outgoing).wait_send()
 
         for d, other in enumerate(partners):
             peer_copy(h, d, other).wait()
@@ -248,7 +267,7 @@
     def block(rows, width, first=0):
         return pl.BlockSpec((rows, width), lambda i: (0, first + i))
 
-    rates = pl.BlockSpec((1, ratio, length), lambda i: (i, 0, 0))
+    rates = pl.BlockSpec((value_heads, length), lambda i: (0, 0))
     mats = pl.BlockSpec((ratio, dim, dim), lambda i: (i, 0, 0))
     mat_shape = jax.ShapeDtypeStruct((value_heads, dim, dim), f32)
     wide_shape = jax.ShapeDtypeStruct((length, value_heads * dim), f32)
@@ -270,8 +289,17 @@
         compiler_params=pltpu.CompilerParams(vmem_limit_bytes=48 * 1024 * 1024),
         name="local",
     )(
-        query_in, key_in, value_in, tails, tails, tails, query_taps, key_taps, value_taps,
-        log_decay.reshape(key_heads, ratio, length), beta_logit.reshape(key_heads, ratio, length),
+        *[
+            pltpu.with_memory_space_constraint(array, pltpu.HBM)
+            for array in (query_in, key_in, value_in)
+        ],
+        tails, tails, tails,
+        *[
+            pltpu.with_memory_space_constraint(array, pltpu.HBM)
+            for array in (
+                query_taps, key_taps, value_taps, log_decay, beta_logit,
+            )
+        ],
     )
 
     ring, peers = lax.axis_size("ctx"), lax.axis_size("head")
@@ -285,6 +313,7 @@
             pltpu.VMEM((value_heads, dim, dim), f32),
             pltpu.VMEM((value_heads, dim, dim), f32),
             pltpu.VMEM((value_heads, length, dim), bf16),
+            pltpu.VMEM((value_heads, length, dim), f32),
             pltpu.SemaphoreType.DMA((value_heads,)),
             pltpu.SemaphoreType.DMA((value_heads,)),
             pltpu.SemaphoreType.DMA((value_heads, peers - 1)),

time: 86.2 us -> 78.7 us (0.913)
  local copies, waits for them, and re-layouts: 11.7 us -> 3.27 us
  waiting for transfers between devices: 2.24 us -> 3.71 us
    unnamed x19 -> x5, local copies, waits for them, and re-layouts: 7.99 us -> 0.98 us
    ppermute x1, waiting for transfers between devices: 2.24 us -> 3.71 us  [shifted(): lax.ppermute(value, axis, [(source, source + steps) for source in range(f...]
    reshape x2 -> x0, local copies, waits for them, and re-layouts: 1.47 us -> none  [the longest x1 0.73 us: body(): log_decay.reshape(key_heads, ratio, length)]
  transfers between devices with their start and end apart: 1 -> 1, of which waited for: 1 -> 1; matrix products, arithmetic and copies ran while one was open for 2% -> 0% of each run, Pallas kernels for 0% -> 0%
where the time goes in v3:
time: 78.7 us; the launch traced here: 78.3 us
  Pallas kernels  70 us (89%)
  waiting for transfers between devices  3.71 us (5%)
  local copies, waits for them, and re-layouts  3.27 us (4%)
  starting transfers between devices  1.29 us (2%)
    pallas_call x1, Pallas kernels, body(): pl.pallas_call(functools.partial(carry_kernel, ring, peers), in_specs=[wh...  42.3 us
    pallas_call x1, Pallas kernels, body(): pl.pallas_call(local_kernel, grid=(key_heads,), in_specs=[block(length, d...  27.7 us
    ppermute x1, waiting for transfers between devices, shifted(): lax.ppermute(value, axis, [(source, source + steps) for source in range(f...  3.71 us
  transfers between devices with their start and end apart: 1, of which 1 were waited for; matrix products, arithmetic and copies ran while one was open for 0% of the time, Pallas kernels for 0%

profile of v3, /device:TPU:27, one launch (start us, length us, event | category | flops | bytes accessed | tf_op | source)
XLA Modules:
  0.0 78.3 jit_solution(6195103507801326661)
XLA Ops:
  0.0 0.0 copy-start.1
  0.0 0.0 copy-start
  0.0 0.8 %slice.9 = bf16[16,512]{1,0:T(8,128)(2,1)S(1)} slice(bf16[512,512]{1,0:T(8,128)(2,1)} %q_ref.1), slice={[496:512], [0:512]} | slice | bytes 32768 | tf_op jit(solution)/shard_map/slice | solution.py:263
  0.8 0.7 slice.10
  1.5 0.8 slice.11
  2.3 1.3 %collective-permute-start = (bf16[16,2048]{1,0:T(8,128)(2,1)S(1)}, bf16[16,2048]{1,0:T(8,128)(2,1)S(1)}, u32[]{:S(2)}, u32[]{:S(2)}) collective-permute-start(bf16[16,2048]{1,0:T(8,128)(2,1)S(1)} %pad_maximum_fusion), channel_id=1, source_target_pairs={{0,4},{4,8},{8,12},{12,16},{16,20},{20,24},{24,28},{1,5},{5,9},{9,... | collective-permute-start | bytes 196616 | tf_op jit(solution)/shard_map/ppermute | solution.py:249
  3.6 3.7 %collective-permute-done.qt_ref.kt_ref.vt_ref = bf16[16,2048]{1,0:T(8,128)(2,1)S(1)} collective-permute-done((bf16[16,2048]{1,0:T(8,128)(2,1)S(1)}, bf16[16,2048]{1,0:T(8,128)(2,1)S(1)}, u32[]{:S(2)}, u32[]{:S(2)}) %collective-permute-start) | collective-permute-done | bytes 65568 | tf_op jit(solution)/shard_map/ppermute | solution.py:249
  7.3 27.7 %local.1 = (f32[512,1024]{1,0:T(8,128)S(1)}, f32[512,1024]{1,0:T(8,128)S(1)}, f32[8,128,128]{2,1,0:T(8,128)S(1)}, f32[8,128,128]{2,1,0:T(8,128)S(1)}) custom-call(bf16[512,512]{1,0:T(8,128)(2,1)} %q_ref.1, bf16[512,512]{1,0:T(8,128)(2,1)} %k_ref.1, bf16[512,1024]{1,0:T(8,128)(2,1)} %v_ref.1, bf16[16,2048]{1,0:T(8,128)(2,1)S(1)} %collective-permute-done.qt_ref.kt_ref.vt_ref, ...), custom_call_target="tpu_custom_call" | custom-call | tf_op jit(solution)/shard_map/local/pallas_call | solution.py:274
  35.0 0.0 copy-done.1
  35.0 0.0 copy-done
  35.0 42.3 %carry.1 = bf16[128,4096]{1,0:T(8,128)(2,1)S(1)} custom-call(f32[512,1024]{1,0:T(8,128)S(1)} %get-tuple-element.9.out_ref, f32[512,1024]{1,0:T(8,128)S(1)} %get-tuple-element.10.eff_ref, f32[8,128,128]{2,1,0:T(8,128)S(1)} %get-tuple-element.11.state_ref, f32[8,128,128]{2,1,0:T(8,128)S(1)} %get-tuple-element.12.prod_ref, bf16[512,1024]{1,0:T(8,128)(2,1)S(1)} %copy-done, ...), custom_call_target="tpu_custom_call" | custom-call | tf_op jit(solution)/shard_map/carry/pallas_call | solution.py:307
  77.3 1.0 %copy.12 = bf16[128,4096]{1,0:T(8,128)(2,1)} copy(bf16[128,4096]{1,0:T(8,128)(2,1)S(1)} %carry.1) | data formatting | bytes 2097152
  (1 shorter events, 0.0 us)
Async XLA Ops:
  0.0 35.0 %copy-start.1 = (f32[128]{0:T(128)S(1)}, f32[128]{0:T(128)}, u32[]{:S(2)}) copy-start(f32[128]{0:T(128)} %param.19) | copy-start | bytes 1540
  0.0 35.0 %copy-start = (bf16[512,1024]{1,0:T(8,128)(2,1)S(1)}, bf16[512,1024]{1,0:T(8,128)(2,1)}, u32[]{:S(2)}) copy-start(bf16[512,1024]{1,0:T(8,128)(2,1)} %gate_ref.1) | copy-start | bytes 3145732
  2.3 5.0 %collective-permute-start = (bf16[16,2048]{1,0:T(8,128)(2,1)S(1)}, bf16[16,2048]{1,0:T(8,128)(2,1)S(1)}, u32[]{:S(2)}, u32[]{:S(2)}) collective-permute-start(bf16[16,2048]{1,0:T(8,128)(2,1)S(1)} %pad_maximum_fusion), channel_id=1, source_target_pairs={{0,4},{4,8},{8,12},{12,16},{16,20},{20,24},{24,28},{1,5},{5,9},{9,... | collective-permute-start | bytes 196616 | tf_op jit(solution)/shard_map/ppermute | solution.py:249

commit v4 on v3

--- a/solution.py
+++ b/solution.py
@@ -50,13 +50,19 @@
 
 
 def local_kernel(
-    q_ref, k_ref, v_ref, qt_ref, kt_ref, vt_ref, qw_ref, kw_ref, vw_ref, ld_ref, bl_ref,
+    dim, q_ref, k_ref, v_ref, qt_ref, kt_ref, vt_ref, qw_ref, kw_ref, vw_ref, ld_ref, bl_ref,
     out_ref, eff_ref, state_ref, prod_ref, qbuf, vbuf,
 ):
-    length, dim = q_ref.shape
-    ratio = v_ref.shape[1] // dim
-    q_all = (unit(conv(qbuf, qt_ref, q_ref, qw_ref)) * dim ** (-0.5)).astype(bf16)
-    k_all = unit(conv(qbuf, kt_ref, k_ref, kw_ref)).astype(bf16)
+    length = q_ref.shape[0]
+    group = q_ref.shape[1] // dim
+    ratio = v_ref.shape[1] // q_ref.shape[1]
+    q_conv = conv(qbuf, qt_ref, q_ref, qw_ref)
+    k_conv = conv(qbuf, kt_ref, k_ref, kw_ref)
+    q_heads, k_heads = [], []
+    for g in range(group):
+        lanes = slice(g * dim, (g + 1) * dim)
+        q_heads.append((unit(q_conv[:, lanes]) * dim ** (-0.5)).astype(bf16))
+        k_heads.append(unit(k_conv[:, lanes]).astype(bf16))
     v_all = conv(vbuf, vt_ref, v_ref, vw_ref).astype(bf16)
 
     size = CHUNK
@@ -75,32 +81,34 @@
         width *= 2
 
     def rate_rows(ref):
-        first = pl.program_id(0) * ratio
-        return jnp.concatenate([ref[pl.ds(first + h, 1), :] for h in range(ratio)], axis=0)
+        first = pl.program_id(0) * (group * ratio)
+        return jnp.concatenate([ref[pl.ds(first + h, 1), :] for h in range(group * ratio)], axis=0)
 
     beta_all = 1.0 / (1.0 + jnp.exp(-rate_rows(bl_ref)))
     decay_all = rate_rows(ld_ref)
     items = []
+    heads = group * ratio
     for c in range(length // size):
         span = slice(c * size, (c + 1) * size)
-        kc, qc = k_all[span], q_all[span]
-        kf, qf = kc.astype(f32), qc.astype(f32)
-        k_turn = kf.T
-        nt = (((1,), (1,)), ((), ()))
-        gram = lax.dot_general(kc, kc, nt, preferred_element_type=f32)
-        qk = lax.dot_general(qc, kc, nt, preferred_element_type=f32)
         cum = lax.dot_general(
             decay_all[:, span], upper, (((1,), (0,)), ((), ())),
             precision=highest, preferred_element_type=f32,
         )
         stacked = jnp.concatenate(
-            [cum, beta_all[:, span], jnp.zeros((8 - 2 * ratio, size), f32)], axis=0
+            [cum, beta_all[:, span], jnp.zeros((-2 * heads % 8, size), f32)][: 3 if -2 * heads % 8 else 2], axis=0
         )
         turned = stacked.T
-        for h in range(ratio):
+        for h in range(heads):
+            if h % ratio == 0:
+                kc, qc = k_heads[h // ratio][span], q_heads[h // ratio][span]
+                kf, qf = kc.astype(f32), qc.astype(f32)
+                k_turn = kf.T
+                nt = (((1,), (1,)), ((), ()))
+                gram = lax.dot_general(kc, kc, nt, preferred_element_type=f32)
+                qk = lax.dot_general(qc, kc, nt, preferred_element_type=f32)
             cum_row = cum[h : h + 1]
             cum_col = turned[:, h : h + 1]
-            beta_col = turned[:, ratio + h : ratio + h + 1]
+            beta_col = turned[:, heads + h : heads + h + 1]
             last = cum_row[:, size - 1 :]
             mask = jnp.where(inside, jnp.exp(jnp.where(inside, cum_col - cum_row, 0.0)), 0.0)
             low = split(jnp.where(strictly, beta_col * gram * mask, 0.0))
@@ -126,7 +134,7 @@
         it["x"] = it["x"] + dot1(x[0], rest.astype(bf16))
     for it in items:
         it["uw"] = dot3(split(it["x"]), it["rhs"])
-    states = [None] * ratio
+    states = [None] * heads
     for it in items:
         c, h = it["c"], it["h"]
         u, w = it["uw"][:, :dim], it["uw"][:, dim:]
@@ -147,7 +155,7 @@
         span = pl.ds(c * size, size)
         out_ref[span, h * dim : (h + 1) * dim] = out[:, :dim]
         eff_ref[span, h * dim : (h + 1) * dim] = out[:, dim:]
-    for h in range(ratio):
+    for h in range(heads):
         state_ref[h] = states[h][:, :dim]
         prod_ref[h] = states[h][:, dim:]
 
@@ -195,7 +203,8 @@
     @pl.when(me == 0)
     def _():
         def send(h, carry):
-            ring_copy(h, state_ref).start()
+            outgoing[h] = state_ref[h].astype(bf16)
+            ring_copy(h, outgoing).start()
             return carry
 
         lax.fori_loop(0, heads, send, 0)
@@ -212,15 +221,18 @@
         def _():
             ring_copy(h, outgoing).wait_recv()
 
-        state = split(incoming[h])
+        state = incoming[h]
 
         @pl.when((me > 0) & (me < ring - 1))
         def _():
-            outgoing[h] = state_ref[h] + dot3(split(prod_ref[h]), state)
+            high, low = split(prod_ref[h])
+            both = jnp.concatenate([high, low], axis=1)
+            moved = dot1(both, jnp.concatenate([state, state], axis=0))
+            outgoing[h] = (state_ref[h] + moved).astype(bf16)
             ring_copy(h, outgoing).start()
 
         span = head_span(h)
-        core = out_ref[:, span] + dot1(eff_ref[:, span].astype(bf16), state[0])
+        core = out_ref[:, span] + dot1(eff_ref[:, span].astype(bf16), state)
         scale = lax.rsqrt(jnp.mean(core * core, axis=-1, keepdims=True) + norm_eps)
         stage[h] = (core * scale * factor[h]).astype(bf16)
         for d, other in enumerate(partners):
@@ -262,28 +274,30 @@
     tails = shifted(
         jnp.concatenate([query_in[-PAD:], key_in[-PAD:], value_in[-PAD:]], axis=1), "ctx", 1
     )
-    wide = ratio * dim
+    group = 2 if key_heads % 2 == 0 else 1
+    narrow, wide = group * dim, group * ratio * dim
 
     def block(rows, width, first=0):
         return pl.BlockSpec((rows, width), lambda i: (0, first + i))
 
     rates = pl.BlockSpec((value_heads, length), lambda i: (0, 0))
-    mats = pl.BlockSpec((ratio, dim, dim), lambda i: (i, 0, 0))
+    mats = pl.BlockSpec((group * ratio, dim, dim), lambda i: (i, 0, 0))
     mat_shape = jax.ShapeDtypeStruct((value_heads, dim, dim), f32)
     wide_shape = jax.ShapeDtypeStruct((length, value_heads * dim), f32)
     local_out, effect, local_state, product = pl.pallas_call(
-        local_kernel,
-        grid=(key_heads,),
+        functools.partial(local_kernel, dim),
+        grid=(key_heads // group,),
         in_specs=[
-            block(length, dim), block(length, dim), block(length, wide),
-            block(PAD, dim), block(PAD, dim, key_heads), block(PAD, wide, 2 * key_heads // ratio),
-            block(taps, dim), block(taps, dim), block(taps, wide),
+            block(length, narrow), block(length, narrow), block(length, wide),
+            block(PAD, narrow), block(PAD, narrow, key_heads // group),
+            block(PAD, wide, 2 * key_heads // (ratio * group)),
+            block(taps, narrow), block(taps, narrow), block(taps, wide),
             rates, rates,
         ],
         out_specs=[block(length, wide), block(length, wide), mats, mats],
         out_shape=[wide_shape, wide_shape, mat_shape, mat_shape],
         scratch_shapes=[
-            pltpu.VMEM((length + PAD, dim), f32),
+            pltpu.VMEM((length + PAD, narrow), f32),
             pltpu.VMEM((length + PAD, wide), f32),
         ],
         compiler_params=pltpu.CompilerParams(vmem_limit_bytes=48 * 1024 * 1024),
@@ -310,8 +324,8 @@
         out_specs=whole,
         out_shape=jax.ShapeDtypeStruct((length // peers, peers * value_heads * dim), bf16),
         scratch_shapes=[
-            pltpu.VMEM((value_heads, dim, dim), f32),
-            pltpu.VMEM((value_heads, dim, dim), f32),
+            pltpu.VMEM((value_heads, dim, dim), bf16),
+            pltpu.VMEM((value_heads, dim, dim), bf16),
             pltpu.VMEM((value_heads, length, dim), bf16),
             pltpu.VMEM((value_heads, length, dim), f32),
             pltpu.SemaphoreType.DMA((value_heads,)),

time: 78.7 us -> 69.5 us (0.88)
  Pallas kernels: 70 us -> 60.9 us
    pallas_call x1, Pallas kernels: 42.3 us -> 36.2 us  [body(): pl.pallas_call(functools.partial(carry_kernel, ring, peers), in_specs=[wh...]
    pallas_call x1, Pallas kernels: 27.7 us -> 24.7 us  [body(): pl.pallas_call(functools.partial(local_kernel, dim), grid=(key_heads // g...]
where the time goes in v4:
time: 69.5 us; the launch traced here: 69.2 us
  Pallas kernels  60.9 us (88%)
  waiting for transfers between devices  3.71 us (5%)
  local copies, waits for them, and re-layouts  3.27 us (5%)
  starting transfers between devices  1.29 us (2%)
    pallas_call x1, Pallas kernels, body(): pl.pallas_call(functools.partial(carry_kernel, ring, peers), in_specs=[wh...  36.2 us
    pallas_call x1, Pallas kernels, body(): pl.pallas_call(functools.partial(local_kernel, dim), grid=(key_heads // g...  24.7 us
    ppermute x1, waiting for transfers between devices, shifted(): lax.ppermute(value, axis, [(source, source + steps) for source in range(f...  3.71 us
  transfers between devices with their start and end apart: 1, of which 1 were waited for; matrix products, arithmetic and copies ran while one was open for 0% of the time, Pallas kernels for 0%

profile of v4, /device:TPU:27, one launch (start us, length us, event | category | flops | bytes accessed | tf_op | source)
XLA Modules:
  0.0 69.2 jit_solution(7313913111615232649)
XLA Ops:
  0.0 0.0 copy-start.1
  0.0 0.0 copy-start
  0.0 0.8 %slice.9 = bf16[16,512]{1,0:T(8,128)(2,1)S(1)} slice(bf16[512,512]{1,0:T(8,128)(2,1)} %q_ref.1), slice={[496:512], [0:512]} | slice | bytes 32768 | tf_op jit(solution)/shard_map/slice | solution.py:275
  0.8 0.7 %slice.10 = bf16[16,512]{1,0:T(8,128)(2,1)S(1)} slice(bf16[512,512]{1,0:T(8,128)(2,1)} %k_ref.1), slice={[496:512], [0:512]} | slice | bytes 32768 | tf_op jit(solution)/shard_map/slice | solution.py:275
  1.5 0.8 %slice.11 = bf16[16,1024]{1,0:T(8,128)(2,1)S(1)} slice(bf16[512,1024]{1,0:T(8,128)(2,1)} %v_ref.1), slice={[496:512], [0:1024]} | slice | bytes 65536 | tf_op jit(solution)/shard_map/slice | solution.py:275
  2.3 1.3 %collective-permute-start = (bf16[16,2048]{1,0:T(8,128)(2,1)S(1)}, bf16[16,2048]{1,0:T(8,128)(2,1)S(1)}, u32[]{:S(2)}, u32[]{:S(2)}) collective-permute-start(bf16[16,2048]{1,0:T(8,128)(2,1)S(1)} %pad_maximum_fusion), channel_id=1, source_target_pairs={{0,4},{4,8},{8,12},{12,16},{16,20},{20,24},{24,28},{1,5},{5,9},{9,... | collective-permute-start | bytes 196616 | tf_op jit(solution)/shard_map/ppermute | solution.py:261
  3.6 3.7 %collective-permute-done.qt_ref.kt_ref.vt_ref = bf16[16,2048]{1,0:T(8,128)(2,1)S(1)} collective-permute-done((bf16[16,2048]{1,0:T(8,128)(2,1)S(1)}, bf16[16,2048]{1,0:T(8,128)(2,1)S(1)}, u32[]{:S(2)}, u32[]{:S(2)}) %collective-permute-start) | collective-permute-done | bytes 65568 | tf_op jit(solution)/shard_map/ppermute | solution.py:261
  7.3 24.7 %local.1 = (f32[512,1024]{1,0:T(8,128)S(1)}, f32[512,1024]{1,0:T(8,128)S(1)}, f32[8,128,128]{2,1,0:T(8,128)S(1)}, f32[8,128,128]{2,1,0:T(8,128)S(1)}) custom-call(bf16[512,512]{1,0:T(8,128)(2,1)} %q_ref.1, bf16[512,512]{1,0:T(8,128)(2,1)} %k_ref.1, bf16[512,1024]{1,0:T(8,128)(2,1)} %v_ref.1, bf16[16,2048]{1,0:T(8,128)(2,1)S(1)} %collective-permute-done.qt_ref.kt_ref.vt_ref, ...), custom_call_target="tpu_custom_call" | custom-call | tf_op jit(solution)/shard_map/local/pallas_call | solution.py:287
  32.0 0.0 copy-done.1
  32.0 0.0 copy-done
  32.0 36.2 %carry.1 = bf16[128,4096]{1,0:T(8,128)(2,1)S(1)} custom-call(f32[512,1024]{1,0:T(8,128)S(1)} %get-tuple-element.9.out_ref, f32[512,1024]{1,0:T(8,128)S(1)} %get-tuple-element.10.eff_ref, f32[8,128,128]{2,1,0:T(8,128)S(1)} %get-tuple-element.11.state_ref, f32[8,128,128]{2,1,0:T(8,128)S(1)} %get-tuple-element.12.prod_ref, bf16[512,1024]{1,0:T(8,128)(2,1)S(1)} %copy-done, ...), custom_call_target="tpu_custom_call" | custom-call | tf_op jit(solution)/shard_map/carry/pallas_call | solution.py:321
  68.2 1.0 %copy.12 = bf16[128,4096]{1,0:T(8,128)(2,1)} copy(bf16[128,4096]{1,0:T(8,128)(2,1)S(1)} %carry.1) | data formatting | bytes 2097152
  (1 shorter events, 0.0 us)
Async XLA Ops:
  0.0 32.0 %copy-start.1 = (f32[128]{0:T(128)S(1)}, f32[128]{0:T(128)}, u32[]{:S(2)}) copy-start(f32[128]{0:T(128)} %param.19) | copy-start | bytes 1540
  0.0 32.0 %copy-start = (bf16[512,1024]{1,0:T(8,128)(2,1)S(1)}, bf16[512,1024]{1,0:T(8,128)(2,1)}, u32[]{:S(2)}) copy-start(bf16[512,1024]{1,0:T(8,128)(2,1)} %gate_ref.1) | copy-start | bytes 3145732
  2.3 5.0 %collective-permute-start = (bf16[16,2048]{1,0:T(8,128)(2,1)S(1)}, bf16[16,2048]{1,0:T(8,128)(2,1)S(1)}, u32[]{:S(2)}, u32[]{:S(2)}) collective-permute-start(bf16[16,2048]{1,0:T(8,128)(2,1)S(1)} %pad_maximum_fusion), channel_id=1, source_target_pairs={{0,4},{4,8},{8,12},{12,16},{16,20},{20,24},{24,28},{1,5},{5,9},{9,... | collective-permute-start | bytes 196616 | tf_op jit(solution)/shard_map/ppermute | solution.py:261

commit v5 on v4

--- a/solution.py
+++ b/solution.py
@@ -144,8 +144,8 @@
             seen = jnp.concatenate([zero, it["qd"]], axis=1)
             kept = jnp.concatenate([jnp.zeros((dim, dim), f32), it["keep"] * eye], axis=1)
         else:
-            both = split(jnp.concatenate([w, it["qd"]], axis=0))
-            got = dot3(both, split(states[h]))
+            both = jnp.concatenate([w, it["qd"]], axis=0).astype(bf16)
+            got = dot1(both, states[h].astype(bf16))
             new = jnp.concatenate([u, zero], axis=1) - got[:size]
             seen = got[size:]
             kept = it["keep"] * states[h]

time: 69.5 us -> 68 us (0.978)
  Pallas kernels: 60.9 us -> 59.4 us
    pallas_call x1, Pallas kernels: 24.7 us -> 23.2 us  [body(): pl.pallas_call(functools.partial(local_kernel, dim), grid=(key_heads // g...]
where the time goes in v5:
time: 68 us; the launch traced here: 67.7 us
  Pallas kernels  59.4 us (87%)
  waiting for transfers between devices  3.71 us (5%)
  local copies, waits for them, and re-layouts  3.27 us (5%)
  starting transfers between devices  1.29 us (2%)
    pallas_call x1, Pallas kernels, body(): pl.pallas_call(functools.partial(carry_kernel, ring, peers), in_specs=[wh...  36.2 us
    pallas_call x1, Pallas kernels, body(): pl.pallas_call(functools.partial(local_kernel, dim), grid=(key_heads // g...  23.2 us
    ppermute x1, waiting for transfers between devices, shifted(): lax.ppermute(value, axis, [(source, source + steps) for source in range(f...  3.71 us
  transfers between devices with their start and end apart: 1, of which 1 were waited for; matrix products, arithmetic and copies ran while one was open for 0% of the time, Pallas kernels for 0%

profile of v5, /device:TPU:27, one launch (start us, length us, event | category | flops | bytes accessed | tf_op | source)
XLA Modules:
  0.0 67.7 jit_solution(8386006720032252535)
XLA Ops:
  0.0 0.0 copy-start.1
  0.0 0.0 copy-start
  0.0 0.8 %slice.9 = bf16[16,512]{1,0:T(8,128)(2,1)S(1)} slice(bf16[512,512]{1,0:T(8,128)(2,1)} %q_ref.1), slice={[496:512], [0:512]} | slice | bytes 32768 | tf_op jit(solution)/shard_map/slice | solution.py:275
  0.8 0.7 %slice.10 = bf16[16,512]{1,0:T(8,128)(2,1)S(1)} slice(bf16[512,512]{1,0:T(8,128)(2,1)} %k_ref.1), slice={[496:512], [0:512]} | slice | bytes 32768 | tf_op jit(solution)/shard_map/slice | solution.py:275
  1.5 0.8 %slice.11 = bf16[16,1024]{1,0:T(8,128)(2,1)S(1)} slice(bf16[512,1024]{1,0:T(8,128)(2,1)} %v_ref.1), slice={[496:512], [0:1024]} | slice | bytes 65536 | tf_op jit(solution)/shard_map/slice | solution.py:275
  2.3 1.3 %collective-permute-start = (bf16[16,2048]{1,0:T(8,128)(2,1)S(1)}, bf16[16,2048]{1,0:T(8,128)(2,1)S(1)}, u32[]{:S(2)}, u32[]{:S(2)}) collective-permute-start(bf16[16,2048]{1,0:T(8,128)(2,1)S(1)} %pad_maximum_fusion), channel_id=1, source_target_pairs={{0,4},{4,8},{8,12},{12,16},{16,20},{20,24},{24,28},{1,5},{5,9},{9,... | collective-permute-start | bytes 196616 | tf_op jit(solution)/shard_map/ppermute | solution.py:261
  3.6 3.7 %collective-permute-done.qt_ref.kt_ref.vt_ref = bf16[16,2048]{1,0:T(8,128)(2,1)S(1)} collective-permute-done((bf16[16,2048]{1,0:T(8,128)(2,1)S(1)}, bf16[16,2048]{1,0:T(8,128)(2,1)S(1)}, u32[]{:S(2)}, u32[]{:S(2)}) %collective-permute-start) | collective-permute-done | bytes 65568 | tf_op jit(solution)/shard_map/ppermute | solution.py:261
  7.3 23.2 %local.1 = (f32[512,1024]{1,0:T(8,128)S(1)}, f32[512,1024]{1,0:T(8,128)S(1)}, f32[8,128,128]{2,1,0:T(8,128)S(1)}, f32[8,128,128]{2,1,0:T(8,128)S(1)}) custom-call(bf16[512,512]{1,0:T(8,128)(2,1)} %q_ref.1, bf16[512,512]{1,0:T(8,128)(2,1)} %k_ref.1, bf16[512,1024]{1,0:T(8,128)(2,1)} %v_ref.1, bf16[16,2048]{1,0:T(8,128)(2,1)S(1)} %collective-permute-done.qt_ref.kt_ref.vt_ref, ...), custom_call_target="tpu_custom_call" | custom-call | tf_op jit(solution)/shard_map/local/pallas_call | solution.py:287
  30.5 0.0 copy-done.1
  30.5 0.0 copy-done
  30.5 36.2 %carry.1 = bf16[128,4096]{1,0:T(8,128)(2,1)S(1)} custom-call(f32[512,1024]{1,0:T(8,128)S(1)} %get-tuple-element.9.out_ref, f32[512,1024]{1,0:T(8,128)S(1)} %get-tuple-element.10.eff_ref, f32[8,128,128]{2,1,0:T(8,128)S(1)} %get-tuple-element.11.state_ref, f32[8,128,128]{2,1,0:T(8,128)S(1)} %get-tuple-element.12.prod_ref, bf16[512,1024]{1,0:T(8,128)(2,1)S(1)} %copy-done, ...), custom_call_target="tpu_custom_call" | custom-call | tf_op jit(solution)/shard_map/carry/pallas_call | solution.py:321
  66.7 1.0 %copy.12 = bf16[128,4096]{1,0:T(8,128)(2,1)} copy(bf16[128,4096]{1,0:T(8,128)(2,1)S(1)} %carry.1) | data formatting | bytes 2097152
  (1 shorter events, 0.0 us)
Async XLA Ops:
  0.0 30.5 %copy-start.1 = (f32[128]{0:T(128)S(1)}, f32[128]{0:T(128)}, u32[]{:S(2)}) copy-start(f32[128]{0:T(128)} %param.19) | copy-start | bytes 1540
  0.0 30.5 %copy-start = (bf16[512,1024]{1,0:T(8,128)(2,1)S(1)}, bf16[512,1024]{1,0:T(8,128)(2,1)}, u32[]{:S(2)}) copy-start(bf16[512,1024]{1,0:T(8,128)(2,1)} %gate_ref.1) | copy-start | bytes 3145732
  2.3 5.0 %collective-permute-start = (bf16[16,2048]{1,0:T(8,128)(2,1)S(1)}, bf16[16,2048]{1,0:T(8,128)(2,1)S(1)}, u32[]{:S(2)}, u32[]{:S(2)}) collective-permute-start(bf16[16,2048]{1,0:T(8,128)(2,1)S(1)} %pad_maximum_fusion), channel_id=1, source_target_pairs={{0,4},{4,8},{8,12},{12,16},{16,20},{20,24},{24,28},{1,5},{5,9},{9,... | collective-permute-start | bytes 196616 | tf_op jit(solution)/shard_map/ppermute | solution.py:261
